TPU v7x, 512 devices: a whole 4x8x8 slice. The times are simulated.
512 devices in a mesh: ctx: 64 (over x, z, core), ch: 8 (over y).
Axes of the slice: x: 4, y: 8, z: 8, core: 2. Of those that a mesh axis runs over, the one named last changes fastest.
Arguments:
- q_in: bfloat16 [8192, 4096], P('ctx', 'ch'), may hold values from -6 to 6
- k_in: bfloat16 [8192, 4096], P('ctx', 'ch'), may hold values from -6 to 6
- v_in: bfloat16 [8192, 4096], P('ctx', 'ch'), may hold values from -6 to 6
- grad_out: bfloat16 [8192, 4096], P('ctx', 'ch'), may hold values from -30 to 30
- short_filter: float32 [3, 4096], P(None, 'ch'), may hold values from -3 to 3
- kernel: float32 [8192, 4096], P('ctx', 'ch'), may hold values from -0.0625 to 0.0625
- skip: float32 [4096], P('ch'), may hold values from -3 to 3
Outputs:
- mixed: bfloat16 [8192, 4096], P('ctx', 'ch')
- grad_q: bfloat16 [8192, 4096], P('ctx', 'ch')
- grad_k: bfloat16 [8192, 4096], P('ctx', 'ch')
- grad_v: bfloat16 [8192, 4096], P('ctx', 'ch')
- grad_short: float32 [3, 4096], P(None, 'ch')
- grad_skip: float32 [4096], P('ch')
- grad_kernel: float32 [8192, 4096], P('ctx', 'ch')
All inputs are finite; a program needn't handle non-finite values.
Results may differ from a plain program's by a relative error of at most 0.009.
Values may be sent and summed in bfloat16 or wider, within the bound.
A program may use at most 64 MiB of HBM per device.

v0:
```python
import math

import jax
import jax.numpy as jnp
from jax import lax
from jax.sharding import PartitionSpec as P

highest = lax.Precision.HIGHEST


def shifted(shard, axis, by):
    size = lax.axis_size(axis)
    pairs = [(i, i + by) for i in range(size) if 0 <= i + by < size]
    return lax.ppermute(shard, axis, pairs)


def phase(left_idx, right_idx, period):
    product = left_idx[:, None] * right_idx[None, :] % period
    return product.astype(jnp.float32) * (2.0 * math.pi / period)


def forward_table(angle):
    cosine = jnp.cos(angle)
    sine = jnp.sin(angle)
    return jnp.stack([jnp.stack([cosine, sine]), jnp.stack([-sine, cosine])])


def inverse_table(angle):
    cosine = jnp.cos(angle)
    sine = jnp.sin(angle)
    return jnp.stack([jnp.stack([cosine, -sine]), jnp.stack([sine, cosine])])


def short_forward(extended, short_taps, rows_here):
    halo_rows = short_taps.shape[0] - 1
    result = short_taps[0] * extended[halo_rows : halo_rows + rows_here]
    for shift_idx in range(1, short_taps.shape[0]):
        result = (
            result
            + short_taps[shift_idx]
            * extended[halo_rows - shift_idx : halo_rows - shift_idx + rows_here]
        )
    return result


def short_backward(extended, short_taps, rows_here):
    result = short_taps[0] * extended[0:rows_here]
    for shift_idx in range(1, short_taps.shape[0]):
        result = result + short_taps[shift_idx] * extended[shift_idx : shift_idx + rows_here]
    return result


def spread_rows(signal, pieces):
    return lax.all_to_all(
        signal.reshape(pieces, signal.shape[0] // pieces, signal.shape[1]),
        "ctx",
        split_axis=0,
        concat_axis=0,
        tiled=True,
    )


def spectrum_tiles(section_in, here_idx, pieces):
    signals, _, slice_rows, channels = section_in.shape
    rows_here = pieces * slice_rows
    fft_len = 2 * pieces * rows_here
    outer_angle = phase(jnp.arange(2 * pieces), jnp.arange(pieces), 2 * pieces)
    outer_table = jnp.stack([jnp.cos(outer_angle), -jnp.sin(outer_angle)])
    part = jnp.einsum("pba,garc->pgbrc", outer_table, section_in, precision=highest)
    part_re = part[0]
    part_im = part[1]
    twist_angle = phase(
        jnp.arange(2 * pieces), here_idx * slice_rows + jnp.arange(slice_rows), fft_len
    )
    twist_cos = jnp.cos(twist_angle)[None, :, :, None]
    twist_sin = jnp.sin(twist_angle)[None, :, :, None]
    turn_re = part_re * twist_cos + part_im * twist_sin
    turn_im = part_im * twist_cos - part_re * twist_sin
    stacked = jnp.stack([turn_re, turn_im]).reshape(2, signals, pieces, 2, slice_rows, channels)
    arrived = lax.all_to_all(stacked, "ctx", split_axis=2, concat_axis=4, tiled=True).reshape(
        2, signals, 2, rows_here, channels
    )
    inner_angle = phase(jnp.arange(rows_here), jnp.arange(rows_here), rows_here)
    spec = jnp.einsum("pqer,qgjrc->pgjec", forward_table(inner_angle), arrived, precision=highest)
    return (spec[0], spec[1])


def rows_from_spectrum(spec_re, spec_im, here_idx, pieces):
    signals, _, rows_here, channels = spec_re.shape
    slice_rows = rows_here // pieces
    fft_len = 2 * pieces * rows_here
    inner_angle = phase(jnp.arange(rows_here), jnp.arange(rows_here), rows_here)
    part = jnp.einsum(
        "pqre,qgjec->pgjrc",
        inverse_table(inner_angle),
        jnp.stack([spec_re, spec_im]),
        precision=highest,
    )
    part_re = part[0]
    part_im = part[1]
    twist_angle = phase(2 * here_idx + jnp.arange(2), jnp.arange(rows_here), fft_len)
    twist_cos = jnp.cos(twist_angle)[None, :, :, None]
    twist_sin = jnp.sin(twist_angle)[None, :, :, None]
    turn_re = part_re * twist_cos - part_im * twist_sin
    turn_im = part_im * twist_cos + part_re * twist_sin
    stacked = jnp.stack([turn_re, turn_im]).reshape(2, signals, 2, pieces, slice_rows, channels)
    arrived = lax.all_to_all(stacked, "ctx", split_axis=3, concat_axis=2, tiled=True).reshape(
        2, signals, 2 * pieces, slice_rows, channels
    )
    outer_angle = phase(jnp.arange(pieces), jnp.arange(2 * pieces), 2 * pieces)
    outer_table = jnp.stack([jnp.cos(outer_angle), -jnp.sin(outer_angle)])
    time_rows = jnp.einsum("qab,qgbrc->garc", outer_table, arrived, precision=highest) / fft_len
    returned = lax.all_to_all(time_rows, "ctx", split_axis=1, concat_axis=1, tiled=True)
    return returned.reshape(signals, rows_here, channels)


def body(q_in, k_in, v_in, grad_out, short_filter, kernel, skip):
    pieces = lax.axis_size("ctx")
    here_idx = lax.axis_index("ctx")
    rows_here, channels = q_in.shape
    seq_len = pieces * rows_here
    halo_rows = short_filter.shape[0] - 1
    lead = shifted(
        (
            q_in[rows_here - halo_rows :],
            k_in[rows_here - halo_rows :],
            v_in[rows_here - halo_rows :],
        ),
        "ctx",
        1,
    )
    q_ext = jnp.concatenate([lead[0], q_in], axis=0).astype(jnp.float32)
    k_ext = jnp.concatenate([lead[1], k_in], axis=0).astype(jnp.float32)
    v_ext = jnp.concatenate([lead[2], v_in], axis=0).astype(jnp.float32)
    q_short = short_forward(q_ext, short_filter, rows_here)
    k_short = short_forward(k_ext, short_filter, rows_here)
    v_short = short_forward(v_ext, short_filter, rows_here)
    product = (k_short * v_short).astype(jnp.bfloat16)
    product_wide = product.astype(jnp.float32)
    slice_rows = rows_here // pieces
    kernel_tiles = lax.all_to_all(
        kernel.reshape(pieces, slice_rows, channels), "ctx", split_axis=0, concat_axis=0, tiled=True
    )
    product_tiles = spread_rows(product, pieces).astype(jnp.float32)
    spec_re, spec_im = spectrum_tiles(jnp.stack([product_tiles, kernel_tiles]), here_idx, pieces)
    signal_re = spec_re[0]
    signal_im = spec_im[0]
    kernel_re = spec_re[1]
    kernel_im = spec_im[1]
    conv_re = signal_re * kernel_re - signal_im * kernel_im
    conv_im = signal_re * kernel_im + signal_im * kernel_re
    conv = rows_from_spectrum(conv_re[None], conv_im[None], here_idx, pieces)[0]
    filtered = conv + skip[None, :] * product_wide
    mixed = (q_short * filtered).astype(jnp.bfloat16)
    upstream = grad_out.astype(jnp.float32)
    back_q = upstream * filtered
    back_mix = upstream * q_short
    back_cast = back_mix.astype(jnp.bfloat16)
    cotan_tiles = spread_rows(back_cast, pieces).astype(jnp.float32)
    cotan_re, cotan_im = spectrum_tiles(cotan_tiles[None], here_idx, pieces)
    grad_re = cotan_re[0]
    grad_im = cotan_im[0]
    corr_re = kernel_re * grad_re + kernel_im * grad_im
    corr_im = kernel_re * grad_im - kernel_im * grad_re
    lag_re = signal_re * grad_re + signal_im * grad_im
    lag_im = signal_re * grad_im - signal_im * grad_re
    returned = rows_from_spectrum(
        jnp.stack([corr_re, lag_re]), jnp.stack([corr_im, lag_im]), here_idx, pieces
    )
    correlate = returned[0]
    kernel_grad = returned[1]
    back_prod = correlate + skip[None, :] * back_mix
    back_k = back_prod * v_short
    back_v = back_prod * k_short
    tail = shifted((back_q[:halo_rows], back_k[:halo_rows], back_v[:halo_rows]), "ctx", -1)
    grad_q = short_backward(
        jnp.concatenate([back_q, tail[0]], axis=0), short_filter, rows_here
    ).astype(jnp.bfloat16)
    grad_k = short_backward(
        jnp.concatenate([back_k, tail[1]], axis=0), short_filter, rows_here
    ).astype(jnp.bfloat16)
    grad_v = short_backward(
        jnp.concatenate([back_v, tail[2]], axis=0), short_filter, rows_here
    ).astype(jnp.bfloat16)
    tap_rows = []
    for shift_idx in range(short_filter.shape[0]):
        first = halo_rows - shift_idx
        tap_rows.append(
            jnp.sum(
                back_q * q_ext[first : first + rows_here]
                + back_k * k_ext[first : first + rows_here]
                + back_v * v_ext[first : first + rows_here],
                axis=0,
            )
        )
    short_grad = jnp.stack(tap_rows)
    skip_grad = jnp.sum(back_mix * product_wide, axis=0)
    kernel_square = jnp.sum(kernel_grad * kernel_grad)
    summed = lax.psum((short_grad, skip_grad, kernel_square), "ctx")
    local_square = jnp.sum(summed[0] * summed[0]) + jnp.sum(summed[1] * summed[1]) + summed[2]
    norm_sq = lax.psum(local_square, "ch")
    clip_limit = math.sqrt(float(seq_len * channels * lax.axis_size("ch")))
    factor = clip_limit / jnp.maximum(jnp.sqrt(norm_sq), clip_limit)
    return (
        mixed,
        grad_q,
        grad_k,
        grad_v,
        factor * summed[0],
        factor * summed[1],
        factor * kernel_grad,
    )


def solution(mesh):
    in_specs = (
        P("ctx", "ch"),
        P("ctx", "ch"),
        P("ctx", "ch"),
        P("ctx", "ch"),
        P(None, "ch"),
        P("ctx", "ch"),
        P("ch"),
    )
    out_specs = (
        P("ctx", "ch"),
        P("ctx", "ch"),
        P("ctx", "ch"),
        P("ctx", "ch"),
        P(None, "ch"),
        P("ch"),
        P("ctx", "ch"),
    )
    return jax.shard_map(body, mesh=mesh, in_specs=in_specs, out_specs=out_specs, check_vma=False)
```

profile of v0, /device:TPU:1, one launch (start us, length us, event | category | flops | bytes accessed | tf_op | source)
XLA Modules:
  0.0 605.5 jit_solution(6001677519297526203)
XLA Ops:
  1.3 5.4 collective-permute-start.2
  10.1 4.4 collective-permute-start
  20.9 13.8 %all-to-all-start = ((bf16[64,2,512]{2,1,0:T(2,128)(2,1)}), bf16[64,2,512]{2,1,0:T(2,128)(2,1)S(1)}, u32[]{:S(2)}, u32[]{:S(2)}) async-start(bf16[64,2,512]{2,1,0:T(2,128)(2,1)} %reshape.558), calls=%async_computation | async-start | bytes 262144 | tf_op jit(solution)/shard_map/all_to_all | solution.py:54
  35.6 9.4 %all-to-all-done = bf16[64,2,512]{2,1,0:T(2,128)(2,1)S(1)} async-done(((bf16[64,2,512]{2,1,0:T(2,128)(2,1)}), bf16[64,2,512]{2,1,0:T(2,128)(2,1)S(1)}, u32[]{:S(2)}, u32[]{:S(2)}) %all-to-all-start) | async-done | bytes 131104 | tf_op jit(solution)/shard_map/all_to_all | solution.py:54
  45.0 4.9 all-to-all-start.5
  50.9 9.4 %all-to-all-done.5 = bf16[64,2,512]{2,1,0:T(2,128)(2,1)S(1)} async-done(((bf16[64,2,512]{2,1,0:T(2,128)(2,1)}), bf16[64,2,512]{2,1,0:T(2,128)(2,1)S(1)}, u32[]{:S(2)}, u32[]{:S(2)}) %all-to-all-start.5) | async-done | bytes 131104 | tf_op jit(solution)/shard_map/all_to_all | solution.py:54
  60.3 4.9 all-to-all-start.1
  68.8 8.4 %all-to-all-done.1 = f32[64,2,512]{2,1,0:T(2,128)S(1)} async-done(((f32[64,2,512]{2,1,0:T(2,128)}), f32[64,2,512]{2,1,0:T(2,128)S(1)}, u32[]{:S(2)}, u32[]{:S(2)}) %all-to-all-start.1) | async-done | bytes 262176 | tf_op jit(solution)/shard_map/all_to_all | solution.py:141
  77.2 6.7 %all-to-all-start.6 = ((f32[2,1,64,2,2,512]{5,3,4,0,1,2:T(2,128)}), f32[2,1,64,2,2,512]{5,3,4,0,1,2:T(2,128)S(1)}, u32[]{:S(2)}, u32[]{:S(2)}) async-start(f32[2,1,64,2,2,512]{5,3,4,0,1,2:T(2,128)} %copy.108), calls=%async_computation.6 | async-start | bytes 2097152 | tf_op jit(solution)/shard_map/all_to_all | solution.py:80
  87.3 2.8 stack.159
  94.2 2.6 copy.100
  96.7 15.5 %all-to-all-done.6 = f32[2,1,64,2,2,512]{5,3,4,0,1,2:T(2,128)S(1)} async-done(((f32[2,1,64,2,2,512]{5,3,4,0,1,2:T(2,128)}), f32[2,1,64,2,2,512]{5,3,4,0,1,2:T(2,128)S(1)}, u32[]{:S(2)}, u32[]{:S(2)}) %all-to-all-start.6) | async-done | bytes 1048608 | tf_op jit(solution)/shard_map/all_to_all | solution.py:80
  113.3 6.5 %all-to-all-start.2 = ((f32[2,2,64,2,2,512]{5,3,4,1,0,2:T(2,128)}), f32[2,2,64,2,2,512]{5,3,4,1,0,2:T(2,128)S(1)}, u32[]{:S(2)}, u32[]{:S(2)}) async-start(f32[2,2,64,2,2,512]{5,3,4,1,0,2:T(2,128)} %copy.100), calls=%async_computation.2 | async-start | bytes 4194304 | tf_op jit(solution)/shard_map/all_to_all | solution.py:80
  121.2 2.6 copy.73
  126.0 3.3 convolution_bitcast_fusion.1
  129.3 41.6 %all-to-all-done.2 = f32[2,2,64,2,2,512]{5,3,4,1,0,2:T(2,128)S(1)} async-done(((f32[2,2,64,2,2,512]{5,3,4,1,0,2:T(2,128)}), f32[2,2,64,2,2,512]{5,3,4,1,0,2:T(2,128)S(1)}, u32[]{:S(2)}, u32[]{:S(2)}) %all-to-all-start.2) | async-done | bytes 2097184 | tf_op jit(solution)/shard_map/all_to_all | solution.py:80
  171.9 3.4 fusion.4
  187.7 6.4 %all-to-all-start.3 = ((f32[2,1,2,64,2,512]{5,4,2,1,0,3:T(2,128)}), f32[2,1,2,64,2,512]{5,4,2,1,0,3:T(2,128)}, u32[]{:S(2)}, u32[]{:S(2)}) async-start(f32[2,1,2,64,2,512]{5,4,2,1,0,3:T(2,128)} %copy.105), calls=%async_computation.3 | async-start | bytes 2097152 | tf_op jit(solution)/shard_map/all_to_all | solution.py:107
  203.7 2.6 copy.112
  206.3 16.1 %all-to-all-done.3 = f32[2,1,2,64,2,512]{5,4,2,1,0,3:T(2,128)} async-done(((f32[2,1,2,64,2,512]{5,4,2,1,0,3:T(2,128)}), f32[2,1,2,64,2,512]{5,4,2,1,0,3:T(2,128)}, u32[]{:S(2)}, u32[]{:S(2)}) %all-to-all-start.3) | async-done | bytes 1048608 | tf_op jit(solution)/shard_map/all_to_all | solution.py:107
  222.4 6.2 %all-to-all-start.7 = ((f32[2,2,2,64,2,512]{5,4,2,1,0,3:T(2,128)}), f32[2,2,2,64,2,512]{5,4,2,1,0,3:T(2,128)S(1)}, u32[]{:S(2)}, u32[]{:S(2)}) async-start(f32[2,2,2,64,2,512]{5,4,2,1,0,3:T(2,128)} %copy.112), calls=%async_computation.7 | async-start | bytes 4194304 | tf_op jit(solution)/shard_map/all_to_all | solution.py:107
  228.8 2.7 copy.68
  231.5 2.9 reshape.562
  237.4 42.5 %all-to-all-done.7 = f32[2,2,2,64,2,512]{5,4,2,1,0,3:T(2,128)S(1)} async-done(((f32[2,2,2,64,2,512]{5,4,2,1,0,3:T(2,128)}), f32[2,2,2,64,2,512]{5,4,2,1,0,3:T(2,128)S(1)}, u32[]{:S(2)}, u32[]{:S(2)}) %all-to-all-start.7) | async-done | bytes 2097184 | tf_op jit(solution)/shard_map/all_to_all | solution.py:107
  279.8 6.2 %all-to-all-start.4 = ((f32[1,64,2,512]{3,2,0,1:T(2,128)}), f32[1,64,2,512]{3,2,0,1:T(2,128)S(1)}, u32[]{:S(2)}, u32[]{:S(2)}) async-start(f32[1,64,2,512]{3,2,0,1:T(2,128)} %copy.69), calls=%async_computation.4 | async-start | bytes 524288 | tf_op jit(solution)/shard_map/all_to_all | solution.py:113
  288.5 2.7 reshape.565
  293.9 4.0 all-to-all-done.4
  297.9 6.3 %all-to-all-start.8 = ((f32[2,64,2,512]{3,2,0,1:T(2,128)}), f32[2,64,2,512]{3,2,0,1:T(2,128)S(1)}, u32[]{:S(2)}, u32[]{:S(2)}) async-start(f32[2,64,2,512]{3,2,0,1:T(2,128)} %copy.83), calls=%async_computation.8 | async-start | bytes 1048576 | tf_op jit(solution)/shard_map/all_to_all | solution.py:113
  304.4 17.1 %all-to-all-done.8 = f32[2,64,2,512]{3,2,0,1:T(2,128)S(1)} async-done(((f32[2,64,2,512]{3,2,0,1:T(2,128)}), f32[2,64,2,512]{3,2,0,1:T(2,128)S(1)}, u32[]{:S(2)}, u32[]{:S(2)}) %all-to-all-start.8) | async-done | bytes 524320 | tf_op jit(solution)/shard_map/all_to_all | solution.py:113
  324.7 242.6 %all-reduce = (f32[3,512]{1,0:T(4,128)S(1)}, f32[512]{0:T(512)S(1)}, f32[]{:T(128)}) all-reduce(f32[3,512]{1,0:T(4,128)S(1)} %pad_maximum_fusion.23, f32[512]{0:T(512)S(1)} %get-tuple-element.13, f32[]{:T(128)} %get-tuple-element.34), channel_id=1, replica_groups=mesh['ctx'=64,'ch'=8] {'ctx'}, use_global_device_ids=true, to_apply=%region_3.4 | all-reduce | flops 2049 | bytes 16392 | tf_op jit(solution)/shard_map/psum | solution.py:199
  570.4 14.4 %psum.31 = f32[]{:T(128)} all-reduce(f32[]{:T(128)S(6)} %add.288), channel_id=1, replica_groups=mesh['ctx'=64,'ch'=8] {'ch'}, use_global_device_ids=true, to_apply=%region_10.11 | all-reduce | flops 1 | bytes 8 | tf_op jit(solution)/shard_map/psum | solution.py:201
  586.1 11.3 %collective-permute-start.3 = (f32[2,512]{1,0:T(2,128)S(1)}, f32[2,512]{1,0:T(2,128)S(1)}, u32[]{:S(2)}, u32[]{:S(2)}) collective-permute-start(f32[2,512]{1,0:T(2,128)S(1)} %slice.213), channel_id=1, source_target_pairs={{8,0},{16,8},{24,16},{32,24},{40,32},{48,40},{56,48},{64,56},{72,6... | collective-permute-start | bytes 12296 | tf_op jit(solution)/shard_map/ppermute | solution.py:14
  (105 shorter events, 71.9 us)
Async XLA Ops:
  1.3 15.8 %collective-permute-start.2 = (bf16[2,512]{1,0:T(2,128)(2,1)S(1)}, bf16[2,512]{1,0:T(2,128)(2,1)S(1)}, u32[]{:S(2)}, u32[]{:S(2)}) collective-permute-start(bf16[2,512]{1,0:T(2,128)(2,1)S(1)} %slice.167), channel_id=1, source_target_pairs={{0,8},{8,16},{16,24},{24,32},{32,40},{40,48},{48,56},{56,64},{64,7... | collective-permute-start | bytes 6152 | tf_op jit(solution)/shard_map/ppermute | solution.py:14
  7.4 8.8 %collective-permute-start.1 = (bf16[2,512]{1,0:T(2,128)(2,1)S(1)}, bf16[2,512]{1,0:T(2,128)(2,1)S(1)}, u32[]{:S(2)}, u32[]{:S(2)}) collective-permute-start(bf16[2,512]{1,0:T(2,128)(2,1)S(1)} %slice.163), channel_id=1, source_target_pairs={{0,8},{8,16},{16,24},{24,32},{32,40},{40,48},{48,56},{56,64},{64,7... | collective-permute-start | bytes 6152 | tf_op jit(solution)/shard_map/ppermute | solution.py:14
  10.1 5.2 collective-permute-start
  18.1 16.7 %copy-start.9 = (bf16[128,512]{1,0:T(8,128)(2,1)S(1)}, bf16[128,512]{1,0:T(8,128)(2,1)}, u32[]{:S(2)}) copy-start(bf16[128,512]{1,0:T(8,128)(2,1)} %param.10) | copy-start | bytes 393220
  18.1 31.8 %copy-start.11 = (f32[128,512]{1,0:T(8,128)S(1)}, f32[128,512]{1,0:T(8,128)}, u32[]{:S(2)}) copy-start(f32[128,512]{1,0:T(8,128)} %param.12) | copy-start | bytes 786436
  20.2 45.6 %copy-start.7 = (bf16[128,512]{1,0:T(8,128)(2,1)}, bf16[128,512]{1,0:T(8,128)(2,1)S(1)}, u32[]{:S(2)}) copy-start(bf16[128,512]{1,0:T(8,128)(2,1)S(1)} %get-tuple-element.14) | copy-start | bytes 393220
  20.9 24.2 %all-to-all-start = ((bf16[64,2,512]{2,1,0:T(2,128)(2,1)}), bf16[64,2,512]{2,1,0:T(2,128)(2,1)S(1)}, u32[]{:S(2)}, u32[]{:S(2)}) async-start(bf16[64,2,512]{2,1,0:T(2,128)(2,1)} %reshape.558), calls=%async_computation | async-start | bytes 262144 | tf_op jit(solution)/shard_map/all_to_all | solution.py:54
  45.0 15.2 %all-to-all-start.5 = ((bf16[64,2,512]{2,1,0:T(2,128)(2,1)}), bf16[64,2,512]{2,1,0:T(2,128)(2,1)S(1)}, u32[]{:S(2)}, u32[]{:S(2)}) async-start(bf16[64,2,512]{2,1,0:T(2,128)(2,1)} %reshape.563), calls=%async_computation.5 | async-start | bytes 262144 | tf_op jit(solution)/shard_map/all_to_all | solution.py:54
  60.3 16.9 %all-to-all-start.1 = ((f32[64,2,512]{2,1,0:T(2,128)}), f32[64,2,512]{2,1,0:T(2,128)S(1)}, u32[]{:S(2)}, u32[]{:S(2)}) async-start(f32[64,2,512]{2,1,0:T(2,128)} %reshape.559), calls=%async_computation.1 | async-start | bytes 524288 | tf_op jit(solution)/shard_map/all_to_all | solution.py:141
  77.2 35.1 %all-to-all-start.6 = ((f32[2,1,64,2,2,512]{5,3,4,0,1,2:T(2,128)}), f32[2,1,64,2,2,512]{5,3,4,0,1,2:T(2,128)S(1)}, u32[]{:S(2)}, u32[]{:S(2)}) async-start(f32[2,1,64,2,2,512]{5,3,4,0,1,2:T(2,128)} %copy.108), calls=%async_computation.6 | async-start | bytes 2097152 | tf_op jit(solution)/shard_map/all_to_all | solution.py:80
  112.3 1.0 copy-start.2
  113.3 57.6 %all-to-all-start.2 = ((f32[2,2,64,2,2,512]{5,3,4,1,0,2:T(2,128)}), f32[2,2,64,2,2,512]{5,3,4,1,0,2:T(2,128)S(1)}, u32[]{:S(2)}, u32[]{:S(2)}) async-start(f32[2,2,64,2,2,512]{5,3,4,1,0,2:T(2,128)} %copy.100), calls=%async_computation.2 | async-start | bytes 4194304 | tf_op jit(solution)/shard_map/all_to_all | solution.py:80
  170.9 0.9 copy-start.5
  170.9 1.0 copy-start.6
  175.3 1.2 copy-start
  187.7 34.7 %all-to-all-start.3 = ((f32[2,1,2,64,2,512]{5,4,2,1,0,3:T(2,128)}), f32[2,1,2,64,2,512]{5,4,2,1,0,3:T(2,128)}, u32[]{:S(2)}, u32[]{:S(2)}) async-start(f32[2,1,2,64,2,512]{5,4,2,1,0,3:T(2,128)} %copy.105), calls=%async_computation.3 | async-start | bytes 2097152 | tf_op jit(solution)/shard_map/all_to_all | solution.py:107
  194.1 1.5 copy-start.1
  194.1 1.7 copy-start.4
  199.9 1.6 copy-start.3
  222.4 57.4 %all-to-all-start.7 = ((f32[2,2,2,64,2,512]{5,4,2,1,0,3:T(2,128)}), f32[2,2,2,64,2,512]{5,4,2,1,0,3:T(2,128)S(1)}, u32[]{:S(2)}, u32[]{:S(2)}) async-start(f32[2,2,2,64,2,512]{5,4,2,1,0,3:T(2,128)} %copy.112), calls=%async_computation.7 | async-start | bytes 4194304 | tf_op jit(solution)/shard_map/all_to_all | solution.py:107
  279.8 18.1 %all-to-all-start.4 = ((f32[1,64,2,512]{3,2,0,1:T(2,128)}), f32[1,64,2,512]{3,2,0,1:T(2,128)S(1)}, u32[]{:S(2)}, u32[]{:S(2)}) async-start(f32[1,64,2,512]{3,2,0,1:T(2,128)} %copy.69), calls=%async_computation.4 | async-start | bytes 524288 | tf_op jit(solution)/shard_map/all_to_all | solution.py:113
  292.7 29.9 %copy-start.8 = (bf16[128,512]{1,0:T(8,128)(2,1)S(1)}, bf16[128,512]{1,0:T(8,128)(2,1)}, u32[]{:S(2)}) copy-start(bf16[128,512]{1,0:T(8,128)(2,1)} %copy-done.7) | copy-start | bytes 393220
  292.7 29.9 %copy-start.10 = (bf16[128,512]{1,0:T(8,128)(2,1)S(1)}, bf16[128,512]{1,0:T(8,128)(2,1)}, u32[]{:S(2)}) copy-start(bf16[128,512]{1,0:T(8,128)(2,1)} %param.10) | copy-start | bytes 393220
  292.7 29.9 %copy-start.12 = (f32[512]{0:T(512)S(1)}, f32[512]{0:T(512)}, u32[]{:S(2)}) copy-start(f32[512]{0:T(512)} %param.13) | copy-start | bytes 6148
  297.9 23.6 %all-to-all-start.8 = ((f32[2,64,2,512]{3,2,0,1:T(2,128)}), f32[2,64,2,512]{3,2,0,1:T(2,128)S(1)}, u32[]{:S(2)}, u32[]{:S(2)}) async-start(f32[2,64,2,512]{3,2,0,1:T(2,128)} %copy.83), calls=%async_computation.8 | async-start | bytes 1048576 | tf_op jit(solution)/shard_map/all_to_all | solution.py:113
  586.1 16.7 %collective-permute-start.3 = (f32[2,512]{1,0:T(2,128)S(1)}, f32[2,512]{1,0:T(2,128)S(1)}, u32[]{:S(2)}, u32[]{:S(2)}) collective-permute-start(f32[2,512]{1,0:T(2,128)S(1)} %slice.213), channel_id=1, source_target_pairs={{8,0},{16,8},{24,16},{32,24},{40,32},{48,40},{56,48},{64,56},{72,6... | collective-permute-start | bytes 12296 | tf_op jit(solution)/shard_map/ppermute | solution.py:14
  597.5 5.4 collective-permute-start.4
  599.4 4.9 collective-permute-start.5
where the time goes:
time: 613 us; the launch traced here: 606 us
  blocking collectives  257 us (42%)
  waiting for transfers between devices  166 us (27%)
  starting transfers between devices  88.6 us (14%)
  local copies, waits for them, and re-layouts  48.5 us (8%)
  other arithmetic  25.9 us (4%)
  matrix products  16 us (3%)
    psum x1, blocking collectives, body(): summed = lax.psum((short_grad, skip_grad, kernel_square), 'ctx')  243 us
    all_to_all x2, waiting for transfers between devices, rows_from_spectrum(): lax.all_to_all(stacked, 'ctx', split_axis=3, concat_axis=2, tiled=True)  58.6 us
    all_to_all x2, waiting for transfers between devices, spectrum_tiles(): lax.all_to_all(stacked, 'ctx', split_axis=2, concat_axis=4, tiled=True)  57.1 us
    ppermute x6, starting transfers between devices, shifted(): return lax.ppermute(shard, axis, pairs)  26.8 us
    all_to_all x2, waiting for transfers between devices, rows_from_spectrum(): lax.all_to_all(time_rows, 'ctx', split_axis=1, concat_axis=1, tiled=True)  21.1 us
    all_to_all x2, waiting for transfers between devices, spread_rows(): lax.all_to_all(signal.reshape(pieces, signal.shape[0] // pieces, signal.s...  18.8 us
    all_to_all x2, starting transfers between devices, spread_rows(): lax.all_to_all(signal.reshape(pieces, signal.shape[0] // pieces, signal.s...  18.7 us
    psum x1, blocking collectives, body(): norm_sq = lax.psum(local_square, 'ch')  14.4 us
  transfers between devices with their start and end apart: 15, of which 10 were waited for; matrix products, arithmetic and copies ran while one was open for 10% of the time, Pallas kernels for 0%

commit v1 on v0

v1 whole, which is shorter than its diff:
```python
import functools
import math

import jax
import jax.numpy as jnp
import numpy as np
from jax import lax
from jax.experimental import pallas as pl
from jax.experimental.pallas import tpu as pltpu
from jax.sharding import PartitionSpec as P

MESH = pl.DeviceIdType.MESH
F32 = jnp.float32
BF16 = jnp.bfloat16
LANES = 128
OWN = 8
HALO, KERN, PROD, BACK, CONV, CORR, LAG, TAIL, SUM1, SUM2, NORM = range(11)


def split_table(table):
    high = table.astype(np.float32).astype(jnp.bfloat16)
    low = (table - high.astype(np.float64)).astype(np.float32).astype(jnp.bfloat16)
    return high, low


def tables(blocks, rows):
    length = blocks * rows
    outer = 2.0 * np.pi * np.outer(np.arange(blocks) + 0.25, np.arange(blocks)) / blocks
    twist = 2.0 * np.pi * np.outer(np.arange(blocks) + 0.25, np.arange(rows)) / length
    inner = 2.0 * np.pi * (np.outer(np.arange(rows), np.arange(rows)) % rows) / rows
    out_f = np.concatenate([np.cos(outer), -np.sin(outer)], axis=0)
    out_i = np.concatenate([np.cos(outer.T), -np.sin(outer.T)], axis=1) / length
    cos, sin = np.cos(inner), np.sin(inner)
    in_f = np.block([[cos, -sin], [sin, cos]])
    in_i = np.block([[cos, sin], [-sin, cos]])
    return (
        np.concatenate(split_table(out_f), axis=1),
        np.concatenate(split_table(out_i), axis=1),
        split_table(in_f)[0],
        split_table(in_i)[0],
        np.cos(twist).astype(np.float32),
        np.sin(twist).astype(np.float32),
    )


def mixer_kernel(
    dims,
    limit,
    q_ref,
    k_ref,
    v_ref,
    go_ref,
    kern_ref,
    taps_ref,
    skip_ref,
    outf_ref,
    outi_ref,
    inf_ref,
    ini_ref,
    tcos_ref,
    tsin_ref,
    mixed_ref,
    gq_ref,
    gk_ref,
    gv_ref,
    gkern_ref,
    small_ref,
    src,
    dst,
    ext,
    wide,
    back,
    hsrc,
    hdst,
    tsrc,
    tdst,
    tmp,
    bbuf,
    spec,
    red,
    red1,
    red2,
    nrm,
    nrmd,
    ssem,
    rsem,
):
    pieces, group_a, group_b, chs = dims
    rows, channels = q_ref.shape
    me = lax.axis_index("ctx")
    ch = lax.axis_index("ch")
    my_a = me // (2 * group_b) * 2 + me % 2
    my_b = me // 2 % group_b

    def ctx_of(a, b):
        return (a // 2 * group_b + b) * 2 + a % 2

    barrier = pltpu.get_barrier_semaphore()

    @pl.loop(1, pieces)
    def _(step):
        peer = lax.rem(me + step, pieces)
        pl.semaphore_signal(barrier, inc=1, device_id=(peer, ch), device_id_type=MESH)

    @pl.loop(1, chs)
    def _(step):
        peer = lax.rem(ch + step, chs)
        pl.semaphore_signal(barrier, inc=1, device_id=(me, peer), device_id_type=MESH)

    def spread(slot):
        @pl.loop(1, pieces)
        def _(step):
            peer = lax.rem(me + step, pieces)
            pltpu.make_async_remote_copy(
                src.at[slot, peer],
                dst.at[slot, me],
                ssem.at[KERN + slot],
                rsem.at[KERN + slot],
                device_id=(peer, ch),
                device_id_type=MESH,
            ).start()

        dst[slot, me] = src[slot, me]

    def arrived(slot):
        view = dst.at[slot, pl.ds(0, pieces - 1)]
        pltpu.make_async_copy(view, view, rsem.at[KERN + slot]).wait()

    def to_pieces(slot, cb, block):
        per = LANES // OWN
        src[slot, cb * per : (cb + 1) * per] = block.T.reshape(per, OWN, rows).astype(BF16)

    def from_pieces(slot, cb):
        per = LANES // OWN
        block = dst[slot, cb * per : (cb + 1) * per].astype(F32)
        return block.reshape(LANES, rows).T

    blocks = [slice(cb * LANES, (cb + 1) * LANES) for cb in range(channels // LANES)]

    for i, ref in enumerate((q_ref, k_ref, v_ref)):
        ext[i, 8 : 8 + rows, :] = ref[...].astype(F32)
        hsrc[2 * i : 2 * i + 2, :] = ext[i, 6 + rows : 8 + rows, :]
    hsrc[6:8, :] = jnp.zeros((2, channels), F32)
    for cb, cs in enumerate(blocks):
        to_pieces(0, cb, kern_ref[:, cs])

    pl.semaphore_wait(barrier, pieces - 1 + chs - 1)

    halo = pltpu.make_async_remote_copy(
        hsrc,
        hdst,
        ssem.at[HALO],
        rsem.at[HALO],
        device_id=(lax.rem(me + 1, pieces), ch),
        device_id_type=MESH,
    )
    halo.start()
    spread(0)
    halo.wait_recv()

    def taps_at(j, cs):
        return taps_ref[j : j + 1, cs]

    def short(i, cs):
        total = taps_at(0, cs) * ext[i, 8 : 8 + rows, cs]
        for j in range(1, 3):
            total = total + taps_at(j, cs) * ext[i, 8 - j : 8 - j + rows, cs]
        return total

    for i in range(3):
        halo_rows = hdst[2 * i : 2 * i + 2, :]
        ext[i, 6:8, :] = jnp.where(me > 0, halo_rows, jnp.zeros_like(halo_rows))
    for cb, cs in enumerate(blocks):
        k_short = short(1, cs)
        v_short = short(2, cs)
        product = (k_short * v_short).astype(BF16).astype(F32)
        wide[1, :, cs] = k_short
        wide[2, :, cs] = v_short
        wide[3, :, cs] = product
        to_pieces(1, cb, product)
    spread(1)
    for cb, cs in enumerate(blocks):
        q_short = short(0, cs)
        back_mix = go_ref[:, cs].astype(F32) * q_short
        wide[0, :, cs] = q_short
        wide[4, :, cs] = back_mix
        red[3:4, cs] = jnp.sum(back_mix * wide[3, :, cs], axis=0, keepdims=True)
        to_pieces(2, cb, back_mix)
    spread(2)

    def transform(slot):
        tmp[...] = dst[slot].astype(F32).reshape(pieces * OWN, rows)
        cols = [tmp[pl.ds(c, pieces, stride=OWN), :] for c in range(OWN)]
        signal = jnp.concatenate(cols, axis=1).astype(BF16)
        part = jnp.dot(
            outf_ref[...],
            jnp.concatenate([signal, signal], axis=0),
            preferred_element_type=F32,
        )
        cos, sin = tcos_ref[...], tsin_ref[...]
        for c in range(OWN):
            re = part[:pieces, c * rows : (c + 1) * rows]
            im = part[pieces:, c * rows : (c + 1) * rows]
            here = slice(c * pieces, (c + 1) * pieces)
            bbuf[here, :rows] = (re * cos + im * sin).astype(BF16)
            bbuf[here, rows:] = (im * cos - re * sin).astype(BF16)
        spec[slot] = jnp.dot(bbuf[...], inf_ref[...], preferred_element_type=F32)

    def inverse(slot, left, right, conj):
        a_re, a_im = spec[left, :, :rows], spec[left, :, rows:]
        b_re, b_im = spec[right, :, :rows], spec[right, :, rows:]
        if conj:
            bbuf[:, :rows] = (a_re * b_re + a_im * b_im).astype(BF16)
            bbuf[:, rows:] = (a_re * b_im - a_im * b_re).astype(BF16)
        else:
            bbuf[:, :rows] = (a_re * b_re - a_im * b_im).astype(BF16)
            bbuf[:, rows:] = (a_re * b_im + a_im * b_re).astype(BF16)
        part = jnp.dot(bbuf[...], ini_ref[...], preferred_element_type=F32)
        cos, sin = tcos_ref[...], tsin_ref[...]
        cols = []
        for c in range(OWN):
            re = part[c * pieces : (c + 1) * pieces, :rows]
            im = part[c * pieces : (c + 1) * pieces, rows:]
            turned = [(re * cos - im * sin).astype(BF16), (im * cos + re * sin).astype(BF16)]
            cols.append(jnp.concatenate(turned, axis=0))
        turned = jnp.concatenate(cols, axis=1)
        out = jnp.dot(
            outi_ref[...],
            jnp.concatenate([turned, turned], axis=0),
            preferred_element_type=F32,
        )
        square = jnp.sum(out * out, axis=0, keepdims=True)
        for c in range(OWN):
            tmp[pl.ds(c, pieces, stride=OWN), :] = out[:, c * rows : (c + 1) * rows]
        src[slot] = tmp[...].reshape(pieces, OWN, rows).astype(BF16)
        return sum(square[:, c * rows : (c + 1) * rows] for c in range(OWN))

    arrived(0)
    transform(0)
    arrived(1)
    transform(1)
    inverse(3, 0, 1, False)
    spread(3)
    arrived(2)
    transform(2)
    inverse(4, 0, 2, True)
    spread(4)
    square = inverse(5, 1, 2, True)
    spread(5)

    red[4:8, :] = jnp.zeros((4, channels), F32)
    red[4:5, :rows] = square

    arrived(3)
    for cb, cs in enumerate(blocks):
        filtered = from_pieces(3, cb) + skip_ref[:, cs] * wide[3, :, cs]
        mixed_ref[:, cs] = (wide[0, :, cs] * filtered).astype(BF16)
        back[0, :rows, cs] = go_ref[:, cs].astype(F32) * filtered
    arrived(4)
    for cb, cs in enumerate(blocks):
        back_prod = from_pieces(4, cb) + skip_ref[:, cs] * wide[4, :, cs]
        back[1, :rows, cs] = back_prod * wide[2, :, cs]
        back[2, :rows, cs] = back_prod * wide[1, :, cs]
        for j in range(3):
            total = back[0, :rows, cs] * ext[0, 8 - j : 8 - j + rows, cs]
            for i in range(1, 3):
                total = total + back[i, :rows, cs] * ext[i, 8 - j : 8 - j + rows, cs]
            red[j : j + 1, cs] = jnp.sum(total, axis=0, keepdims=True)

    @pl.loop(1, group_a)
    def _(step):
        peer = lax.rem(my_a + step, group_a)
        pltpu.make_async_remote_copy(
            red,
            red1.at[my_a],
            ssem.at[SUM1],
            rsem.at[SUM1],
            device_id=(ctx_of(peer, my_b), ch),
            device_id_type=MESH,
        ).start()

    red1[my_a] = red[...]

    for i in range(3):
        tsrc[2 * i : 2 * i + 2, :] = back[i, 0:2, :]
    tsrc[6:8, :] = jnp.zeros((2, channels), F32)
    tail = pltpu.make_async_remote_copy(
        tsrc,
        tdst,
        ssem.at[TAIL],
        rsem.at[TAIL],
        device_id=(lax.rem(me + pieces - 1, pieces), ch),
        device_id_type=MESH,
    )
    tail.start()

    def wait_many(ref, count, sem):
        view = ref.at[pl.ds(0, count)]
        pltpu.make_async_copy(view, view, sem).wait()

    wait_many(red1, group_a - 1, rsem.at[SUM1])
    wait_many(red1, group_a - 1, ssem.at[SUM1])
    total = red1[0]
    for i in range(1, group_a):
        total = total + red1[i]
    red[...] = total

    @pl.loop(1, group_b)
    def _(step):
        peer = lax.rem(my_b + step, group_b)
        pltpu.make_async_remote_copy(
            red,
            red2.at[my_b],
            ssem.at[SUM2],
            rsem.at[SUM2],
            device_id=(ctx_of(my_a, peer), ch),
            device_id_type=MESH,
        ).start()

    red2[my_b] = red[...]

    tail.wait_recv()
    for i, ref in enumerate((gq_ref, gk_ref, gv_ref)):
        tail_rows = tdst[2 * i : 2 * i + 2, :]
        back[i, rows : rows + 2, :] = jnp.where(
            me < pieces - 1, tail_rows, jnp.zeros_like(tail_rows)
        )
        for cs in blocks:
            total = taps_at(0, cs) * back[i, 0:rows, cs]
            for j in range(1, 3):
                total = total + taps_at(j, cs) * back[i, j : j + rows, cs]
            ref[:, cs] = total.astype(BF16)

    wait_many(red2, group_b - 1, rsem.at[SUM2])
    wait_many(red2, group_b - 1, ssem.at[SUM2])
    sums = red2[0]
    for i in range(1, group_b):
        sums = sums + red2[i]
    row = lax.broadcasted_iota(jnp.int32, sums.shape, 0)
    squares = jnp.where(row < 4, sums * sums, sums)
    nrm[...] = jnp.broadcast_to(jnp.sum(squares, keepdims=True), nrm.shape)

    @pl.loop(1, chs)
    def _(step):
        peer = lax.rem(ch + step, chs)
        pltpu.make_async_remote_copy(
            nrm,
            nrmd.at[ch],
            ssem.at[NORM],
            rsem.at[NORM],
            device_id=(me, peer),
            device_id_type=MESH,
        ).start()

    nrmd[ch] = nrm[...]

    arrived(5)
    for cb, cs in enumerate(blocks):
        gkern_ref[:, cs] = from_pieces(5, cb)

    wait_many(nrmd, chs - 1, rsem.at[NORM])
    wait_many(nrmd, chs - 1, ssem.at[NORM])
    norm_sq = nrmd[0]
    for i in range(1, chs):
        norm_sq = norm_sq + nrmd[i]
    factor = limit / jnp.maximum(jnp.sqrt(norm_sq), limit)
    factor = factor[0:1, 0:1]
    small_ref[...] = factor * sums
    gkern_ref[...] = factor * gkern_ref[...]

    halo.wait_send()
    tail.wait_send()
    for slot in range(6):
        view = src.at[slot, pl.ds(0, pieces - 1)]
        pltpu.make_async_copy(view, view, ssem.at[KERN + slot]).wait()


def body(sizes, q_in, k_in, v_in, grad_out, short_filter, kernel, skip):
    pieces, chs = sizes
    rows, channels = q_in.shape
    group_a = group_b = math.isqrt(pieces)
    limit = math.sqrt(float(pieces * rows * channels * chs))
    consts = [jnp.asarray(table) for table in tables(pieces, rows)]
    wide = jax.ShapeDtypeStruct((rows, channels), BF16)
    vmem = pl.BlockSpec(memory_space=pltpu.VMEM)
    mixed, grad_q, grad_k, grad_v, grad_kernel, small = pl.pallas_call(
        functools.partial(mixer_kernel, (pieces, group_a, group_b, chs), limit),
        out_shape=[
            wide,
            wide,
            wide,
            wide,
            jax.ShapeDtypeStruct((rows, channels), F32),
            jax.ShapeDtypeStruct((8, channels), F32),
        ],
        in_specs=[vmem] * 13,
        out_specs=[vmem] * 6,
        scratch_shapes=[
            pltpu.VMEM((6, pieces, OWN, rows), BF16),
            pltpu.VMEM((6, pieces, OWN, rows), BF16),
            pltpu.VMEM((3, rows + 8, channels), F32),
            pltpu.VMEM((5, rows, channels), F32),
            pltpu.VMEM((3, rows + 8, channels), F32),
            pltpu.VMEM((8, channels), F32),
            pltpu.VMEM((8, channels), F32),
            pltpu.VMEM((8, channels), F32),
            pltpu.VMEM((8, channels), F32),
            pltpu.VMEM((pieces * OWN, rows), F32),
            pltpu.VMEM((pieces * OWN, 2 * rows), BF16),
            pltpu.VMEM((3, pieces * OWN, 2 * rows), F32),
            pltpu.VMEM((8, channels), F32),
            pltpu.VMEM((group_a, 8, channels), F32),
            pltpu.VMEM((group_b, 8, channels), F32),
            pltpu.VMEM((8, LANES), F32),
            pltpu.VMEM((chs, 8, LANES), F32),
            pltpu.SemaphoreType.DMA((11,)),
            pltpu.SemaphoreType.DMA((11,)),
        ],
        compiler_params=pltpu.CompilerParams(
            collective_id=0, has_side_effects=True, vmem_limit_bytes=40 << 20
        ),
        name="mixer",
    )(q_in, k_in, v_in, grad_out, kernel, short_filter, skip[None, :], *consts)
    return mixed, grad_q, grad_k, grad_v, small[:3], small[3], grad_kernel


def solution(mesh):
    whole = P("ctx", "ch")
    return jax.shard_map(
        functools.partial(body, (mesh.shape["ctx"], mesh.shape["ch"])),
        mesh=mesh,
        in_specs=(whole, whole, whole, whole, P(None, "ch"), whole, P("ch")),
        out_specs=(whole, whole, whole, whole, P(None, "ch"), P("ch"), whole),
        check_vma=False,
    )
```

time: 613 us -> 69.5 us (0.11); the launches traced: 606 us -> 68.9 us
  blocking collectives: 257 us -> 0 us
  waiting for transfers between devices: 166 us -> 0 us
  starting transfers between devices: 88.6 us -> 0 us
  Pallas kernels: 0 us -> 52.9 us
  local copies, waits for them, and re-layouts: 48.5 us -> 15.3 us
  other arithmetic: 25.9 us -> 0 us
  matrix products: 16 us -> 0 us
    psum x2 -> x0, blocking collectives: 257 us -> none  [the longest x1 243 us: body(): summed = lax.psum((short_grad, skip_grad, kernel_square), 'ctx')]
    all_to_all x9 -> x0, waiting for transfers between devices: 164 us -> none  [the longest x2 58.6 us: rows_from_spectrum(): lax.all_to_all(stacked, 'ctx', split_axis=3, concat_axis=2, tiled=True)]
    all_to_all x9 -> x0, starting transfers between devices: 61.8 us -> none  [the longest x2 18.7 us: spread_rows(): lax.all_to_all(signal.reshape(pieces, signal.shape[0] // pieces, signal.s...]
    pallas_call x0 -> x1, Pallas kernels: none -> 52.9 us  [body(): pl.pallas_call(functools.partial(mixer_kernel, (pieces, group_a, group_b,...]
    ppermute x6 -> x0, starting transfers between devices: 26.8 us -> none  [shifted(): return lax.ppermute(shard, axis, pairs)]
    another operation x15 -> x0, local copies, waits for them, and re-layouts: 26.3 us -> none  [the longest x6 11.7 us: rows_from_spectrum(): jnp.stack([turn_re, turn_im])]
    dot_general x8 -> x0, matrix products: 16 us -> none  [the longest x2 6.76 us: spectrum_tiles(): jnp.einsum('pqer,qgjrc->pgjec', forward_table(inner_angle), arrived, prec...]
    unnamed x26 -> x31, local copies, waits for them, and re-layouts: 2.45 us -> 14.1 us
  transfers between devices with their start and end apart: 15 -> 0, of which waited for: 10 -> 0; matrix products, arithmetic and copies ran while one was open for 10% -> 0% of each run, Pallas kernels for 0% -> 0%
where the time goes in v1:
time: 69.5 us; the launch traced here: 68.9 us
  Pallas kernels  52.9 us (76%)
  local copies, waits for them, and re-layouts  15.3 us (22%)
    pallas_call x1, Pallas kernels, body(): pl.pallas_call(functools.partial(mixer_kernel, (pieces, group_a, group_b,...  52.9 us
    unnamed x31, local copies, waits for them, and re-layouts  14.1 us

profile of v1, /device:TPU:1, one launch (start us, length us, event | category | flops | bytes accessed | tf_op | source)
XLA Modules:
  0.0 68.9 jit_solution(14388987065492168006)
XLA Ops:
  0.6 0.0 copy-start
  0.6 0.9 %copy-done = f32[128,512]{1,0:T(8,128)S(1)} copy-done((f32[128,512]{1,0:T(8,128)S(1)}, f32[128,512]{1,0:T(8,128)}, u32[]{:S(2)}) %copy-start) | copy-done | bytes 262168
  1.6 0.0 copy-start.1
  1.6 0.9 %copy-done.1 = bf16[128,512]{1,0:T(8,128)(2,1)S(1)} copy-done((bf16[128,512]{1,0:T(8,128)(2,1)S(1)}, bf16[128,512]{1,0:T(8,128)(2,1)}, u32[]{:S(2)}) %copy-start.1) | copy-done | bytes 131096
  2.5 0.0 copy-start.2
  2.5 0.9 %copy-done.2 = bf16[128,512]{1,0:T(8,128)(2,1)S(1)} copy-done((bf16[128,512]{1,0:T(8,128)(2,1)S(1)}, bf16[128,512]{1,0:T(8,128)(2,1)}, u32[]{:S(2)}) %copy-start.2) | copy-done | bytes 131096
  3.4 0.0 copy-start.3
  3.4 0.9 %copy-done.3 = bf16[128,512]{1,0:T(8,128)(2,1)S(1)} copy-done((bf16[128,512]{1,0:T(8,128)(2,1)S(1)}, bf16[128,512]{1,0:T(8,128)(2,1)}, u32[]{:S(2)}) %copy-start.3) | copy-done | bytes 131096
  4.3 0.0 copy-start.4
  4.3 0.9 %copy-done.4 = bf16[128,512]{1,0:T(8,128)(2,1)S(1)} copy-done((bf16[128,512]{1,0:T(8,128)(2,1)S(1)}, bf16[128,512]{1,0:T(8,128)(2,1)}, u32[]{:S(2)}) %copy-start.4) | copy-done | bytes 131096
  5.2 0.0 copy-start.5
  5.2 0.9 %copy-done.5 = bf16[256,256]{1,0:T(8,128)(2,1)S(1)} copy-done((bf16[256,256]{1,0:T(8,128)(2,1)S(1)}, bf16[256,256]{1,0:T(8,128)(2,1)}, u32[]{:S(2)}) %copy-start.5) | copy-done | bytes 131096
  6.1 0.0 copy-start.6
  6.1 0.9 %copy-done.6 = bf16[256,256]{1,0:T(8,128)(2,1)S(1)} copy-done((bf16[256,256]{1,0:T(8,128)(2,1)S(1)}, bf16[256,256]{1,0:T(8,128)(2,1)}, u32[]{:S(2)}) %copy-start.6) | copy-done | bytes 131096
  7.0 0.0 copy-start.7
  7.0 0.8 %copy-done.7 = f32[64,128]{1,0:T(8,128)S(1)} copy-done((f32[64,128]{1,0:T(8,128)S(1)}, f32[64,128]{1,0:T(8,128)}, u32[]{:S(2)}) %copy-start.7) | copy-done | bytes 32792
  7.8 0.0 copy-start.8
  7.8 0.8 %copy-done.8 = f32[64,128]{1,0:T(8,128)S(1)} copy-done((f32[64,128]{1,0:T(8,128)S(1)}, f32[64,128]{1,0:T(8,128)}, u32[]{:S(2)}) %copy-start.8) | copy-done | bytes 32792
  8.5 0.0 copy-start.9
  8.5 0.8 %copy-done.9 = bf16[64,256]{1,0:T(8,128)(2,1)S(1)} copy-done((bf16[64,256]{1,0:T(8,128)(2,1)S(1)}, bf16[64,256]{1,0:T(8,128)(2,1)}, u32[]{:S(2)}) %copy-start.9) | copy-done | bytes 32792
  9.3 0.0 copy-start.10
  9.3 0.8 %copy-done.10 = bf16[128,128]{1,0:T(8,128)(2,1)S(1)} copy-done((bf16[128,128]{1,0:T(8,128)(2,1)S(1)}, bf16[128,128]{1,0:T(8,128)(2,1)}, u32[]{:S(2)}) %copy-start.10) | copy-done | bytes 32792
  10.1 0.7 %copy-done.11 = f32[3,512]{1,0:T(4,128)S(1)} copy-done((f32[3,512]{1,0:T(4,128)S(1)}, f32[3,512]{1,0:T(4,128)}, u32[]{:S(2)}) %copy-start.11) | copy-done | bytes 6168
  10.7 0.7 copy-done.12
  11.4 52.9 %mixer.1 = (bf16[128,512]{1,0:T(8,128)(2,1)S(1)}, bf16[128,512]{1,0:T(8,128)(2,1)S(1)}, bf16[128,512]{1,0:T(8,128)(2,1)S(1)}, bf16[128,512]{1,0:T(8,128)(2,1)S(1...) custom-call(bf16[128,512]{1,0:T(8,128)(2,1)S(1)} %copy-done.1, bf16[128,512]{1,0:T(8,128)(2,1)S(1)} %copy-done.2, ...), custom_call_target="tpu_custom_call" | custom-call | tf_op jit(solution)/shard_map/mixer/pallas_call | solution.py:386
  64.4 0.6 slice.7
  65.0 0.6 slice.6
  65.6 0.7 copy.25
  66.2 0.7 copy.26
  66.9 0.7 copy.27
  67.5 0.7 copy.28
  68.2 0.7 %copy.29 = f32[128,512]{1,0:T(8,128)} copy(f32[128,512]{1,0:T(8,128)S(1)} %get-tuple-element.32) | data formatting | bytes 524288
  (2 shorter events, 0.0 us)
Async XLA Ops:
  0.6 1.0 %copy-start = (f32[128,512]{1,0:T(8,128)S(1)}, f32[128,512]{1,0:T(8,128)}, u32[]{:S(2)}) copy-start(f32[128,512]{1,0:T(8,128)} %kern_ref.1) | copy-start | bytes 786436
  1.6 0.9 %copy-start.1 = (bf16[128,512]{1,0:T(8,128)(2,1)S(1)}, bf16[128,512]{1,0:T(8,128)(2,1)}, u32[]{:S(2)}) copy-start(bf16[128,512]{1,0:T(8,128)(2,1)} %q_ref.1) | copy-start | bytes 393220
  2.5 0.9 %copy-start.2 = (bf16[128,512]{1,0:T(8,128)(2,1)S(1)}, bf16[128,512]{1,0:T(8,128)(2,1)}, u32[]{:S(2)}) copy-start(bf16[128,512]{1,0:T(8,128)(2,1)} %k_ref.1) | copy-start | bytes 393220
  3.4 0.9 %copy-start.3 = (bf16[128,512]{1,0:T(8,128)(2,1)S(1)}, bf16[128,512]{1,0:T(8,128)(2,1)}, u32[]{:S(2)}) copy-start(bf16[128,512]{1,0:T(8,128)(2,1)} %v_ref.1) | copy-start | bytes 393220
  4.3 0.9 %copy-start.4 = (bf16[128,512]{1,0:T(8,128)(2,1)S(1)}, bf16[128,512]{1,0:T(8,128)(2,1)}, u32[]{:S(2)}) copy-start(bf16[128,512]{1,0:T(8,128)(2,1)} %go_ref.1) | copy-start | bytes 393220
  5.2 0.9 %copy-start.5 = (bf16[256,256]{1,0:T(8,128)(2,1)S(1)}, bf16[256,256]{1,0:T(8,128)(2,1)}, u32[]{:S(2)}) copy-start(bf16[256,256]{1,0:T(8,128)(2,1)} %constant.15.clone.ini_ref) | copy-start | bytes 393220
  6.1 0.9 %copy-start.6 = (bf16[256,256]{1,0:T(8,128)(2,1)S(1)}, bf16[256,256]{1,0:T(8,128)(2,1)}, u32[]{:S(2)}) copy-start(bf16[256,256]{1,0:T(8,128)(2,1)} %constant.14.clone.inf_ref) | copy-start | bytes 393220
  7.0 0.8 %copy-start.7 = (f32[64,128]{1,0:T(8,128)S(1)}, f32[64,128]{1,0:T(8,128)}, u32[]{:S(2)}) copy-start(f32[64,128]{1,0:T(8,128)} %constant.17.clone.tsin_ref) | copy-start | bytes 98308
  7.8 0.8 %copy-start.8 = (f32[64,128]{1,0:T(8,128)S(1)}, f32[64,128]{1,0:T(8,128)}, u32[]{:S(2)}) copy-start(f32[64,128]{1,0:T(8,128)} %constant.16.clone.tcos_ref) | copy-start | bytes 98308
  8.5 0.8 %copy-start.9 = (bf16[64,256]{1,0:T(8,128)(2,1)S(1)}, bf16[64,256]{1,0:T(8,128)(2,1)}, u32[]{:S(2)}) copy-start(bf16[64,256]{1,0:T(8,128)(2,1)} %constant.13.clone.outi_ref) | copy-start | bytes 98308
  9.3 0.8 %copy-start.10 = (bf16[128,128]{1,0:T(8,128)(2,1)S(1)}, bf16[128,128]{1,0:T(8,128)(2,1)}, u32[]{:S(2)}) copy-start(bf16[128,128]{1,0:T(8,128)(2,1)} %constant.12.clone.outf_ref) | copy-start | bytes 98308
  10.0 0.7 %copy-start.11 = (f32[3,512]{1,0:T(4,128)S(1)}, f32[3,512]{1,0:T(4,128)}, u32[]{:S(2)}) copy-start(f32[3,512]{1,0:T(4,128)} %taps_ref.1) | copy-start | bytes 18436
  10.7 0.7 copy-start.12

commit v2 on v1

--- a/solution.py
+++ b/solution.py
@@ -14,7 +14,7 @@
 BF16 = jnp.bfloat16
 LANES = 128
 OWN = 8
-HALO, KERN, PROD, BACK, CONV, CORR, LAG, TAIL, SUM1, SUM2, NORM = range(11)
+HALO, KERN, PROD, BACK, CONV, CORR, LAG, TAIL, SUM1, SUM2, SUM3, NORM = range(12)
 
 
 def split_table(table):
@@ -46,25 +46,37 @@
 def mixer_kernel(
     dims,
     limit,
-    q_ref,
+    *refs,
+):
+    inputs, refs = refs[:13], refs[13:]
+    outputs, refs = refs[:7], refs[7:]
+    loaded, refs = refs[:13], refs[13:]
+    (
+    kern_ref,
     k_ref,
     v_ref,
+    q_ref,
     go_ref,
-    kern_ref,
     taps_ref,
-    skip_ref,
     outf_ref,
-    outi_ref,
     inf_ref,
-    ini_ref,
     tcos_ref,
     tsin_ref,
+    outi_ref,
+    ini_ref,
+    skip_ref,
+    ) = loaded
+    ready, refs = refs[:7], refs[7:]
+    (
     mixed_ref,
     gq_ref,
     gk_ref,
     gv_ref,
-    gkern_ref,
+    lag_ref,
     small_ref,
+    factor_ref,
+    ) = ready
+    (
     src,
     dst,
     ext,
@@ -77,14 +89,19 @@
     tmp,
     bbuf,
     spec,
-    red,
+    part1,
     red1,
+    part2,
     red2,
+    part3,
+    red3,
     nrm,
     nrmd,
     ssem,
     rsem,
-):
+    isem,
+    osem,
+    ) = refs
     pieces, group_a, group_b, chs = dims
     rows, channels = q_ref.shape
     me = lax.axis_index("ctx")
@@ -95,9 +112,16 @@
     def ctx_of(a, b):
         return (a // 2 * group_b + b) * 2 + a % 2
 
+    loads = [
+        pltpu.make_async_copy(far, near, isem.at[i])
+        for i, (far, near) in enumerate(zip(inputs, loaded))
+    ]
+    for load in loads:
+        load.start()
+
     barrier = pltpu.get_barrier_semaphore()
 
-    @pl.loop(1, pieces)
+    @pl.loop(1, pieces, unroll=9)
     def _(step):
         peer = lax.rem(me + step, pieces)
         pl.semaphore_signal(barrier, inc=1, device_id=(peer, ch), device_id_type=MESH)
@@ -108,7 +132,7 @@
         pl.semaphore_signal(barrier, inc=1, device_id=(me, peer), device_id_type=MESH)
 
     def spread(slot):
-        @pl.loop(1, pieces)
+        @pl.loop(1, pieces, unroll=9)
         def _(step):
             peer = lax.rem(me + step, pieces)
             pltpu.make_async_remote_copy(
@@ -137,12 +161,19 @@
 
     blocks = [slice(cb * LANES, (cb + 1) * LANES) for cb in range(channels // LANES)]
 
-    for i, ref in enumerate((q_ref, k_ref, v_ref)):
+    stores = [
+        pltpu.make_async_copy(near, far, osem.at[i])
+        for i, (near, far) in enumerate(zip(ready, outputs))
+    ]
+
+    loads[0].wait()
+    for cb, cs in enumerate(blocks):
+        to_pieces(0, cb, kern_ref[:, cs])
+    for i, (ref, order) in enumerate(((q_ref, 3), (k_ref, 1), (v_ref, 2))):
+        loads[order].wait()
         ext[i, 8 : 8 + rows, :] = ref[...].astype(F32)
         hsrc[2 * i : 2 * i + 2, :] = ext[i, 6 + rows : 8 + rows, :]
     hsrc[6:8, :] = jnp.zeros((2, channels), F32)
-    for cb, cs in enumerate(blocks):
-        to_pieces(0, cb, kern_ref[:, cs])
 
     pl.semaphore_wait(barrier, pieces - 1 + chs - 1)
 
@@ -156,6 +187,8 @@
     )
     halo.start()
     spread(0)
+    for load in loads[4:]:
+        load.wait()
     halo.wait_recv()
 
     def taps_at(j, cs):
@@ -184,7 +217,7 @@
         back_mix = go_ref[:, cs].astype(F32) * q_short
         wide[0, :, cs] = q_short
         wide[4, :, cs] = back_mix
-        red[3:4, cs] = jnp.sum(back_mix * wide[3, :, cs], axis=0, keepdims=True)
+        part1[2 * cb + 1, 1:2, :] = jnp.sum(back_mix * wide[3, :, cs], axis=0, keepdims=True)
         to_pieces(2, cb, back_mix)
     spread(2)
 
@@ -248,14 +281,15 @@
     square = inverse(5, 1, 2, True)
     spread(5)
 
-    red[4:8, :] = jnp.zeros((4, channels), F32)
-    red[4:5, :rows] = square
+    part2[2:3, :] = square
+    part2[3:4, :] = jnp.zeros_like(square)
 
     arrived(3)
     for cb, cs in enumerate(blocks):
         filtered = from_pieces(3, cb) + skip_ref[:, cs] * wide[3, :, cs]
         mixed_ref[:, cs] = (wide[0, :, cs] * filtered).astype(BF16)
         back[0, :rows, cs] = go_ref[:, cs].astype(F32) * filtered
+    stores[0].start()
     arrived(4)
     for cb, cs in enumerate(blocks):
         back_prod = from_pieces(4, cb) + skip_ref[:, cs] * wide[4, :, cs]
@@ -265,21 +299,41 @@
             total = back[0, :rows, cs] * ext[0, 8 - j : 8 - j + rows, cs]
             for i in range(1, 3):
                 total = total + back[i, :rows, cs] * ext[i, 8 - j : 8 - j + rows, cs]
-            red[j : j + 1, cs] = jnp.sum(total, axis=0, keepdims=True)
-
-    @pl.loop(1, group_a)
-    def _(step):
-        peer = lax.rem(my_a + step, group_a)
-        pltpu.make_async_remote_copy(
-            red,
-            red1.at[my_a],
-            ssem.at[SUM1],
-            rsem.at[SUM1],
-            device_id=(ctx_of(peer, my_b), ch),
-            device_id_type=MESH,
-        ).start()
-
-    red1[my_a] = red[...]
+            here = 2 * cb + j // 2
+            part1[here, j % 2 : j % 2 + 1, :] = jnp.sum(total, axis=0, keepdims=True)
+
+    def exchange(source, slots, mine, size, sem, device_of, own):
+        @pl.loop(1, size, unroll=True)
+        def _(step):
+            peer = lax.rem(mine + step, size)
+            pltpu.make_async_remote_copy(
+                source(peer),
+                slots.at[mine],
+                ssem.at[sem],
+                rsem.at[sem],
+                device_id=device_of(peer),
+                device_id_type=MESH,
+            ).start()
+
+        slots[mine] = own()
+
+    def wait_many(slots, size, sem):
+        view = slots.at[pl.ds(0, size - 1)]
+        pltpu.make_async_copy(view, view, sem).wait()
+
+    def total_of(slots, size, sem):
+        wait_many(slots, size, rsem.at[sem])
+        total = slots[0]
+        for i in range(1, size):
+            total = total + slots[i]
+        return total
+
+    def along_a(peer):
+        return (ctx_of(peer, my_b), ch)
+
+    exchange(
+        lambda peer: part1.at[peer], red1, my_a, group_a, SUM1, along_a, lambda: part1[my_a]
+    )
 
     for i in range(3):
         tsrc[2 * i : 2 * i + 2, :] = back[i, 0:2, :]
@@ -294,30 +348,16 @@
     )
     tail.start()
 
-    def wait_many(ref, count, sem):
-        view = ref.at[pl.ds(0, count)]
-        pltpu.make_async_copy(view, view, sem).wait()
-
-    wait_many(red1, group_a - 1, rsem.at[SUM1])
-    wait_many(red1, group_a - 1, ssem.at[SUM1])
-    total = red1[0]
-    for i in range(1, group_a):
-        total = total + red1[i]
-    red[...] = total
-
-    @pl.loop(1, group_b)
-    def _(step):
-        peer = lax.rem(my_b + step, group_b)
-        pltpu.make_async_remote_copy(
-            red,
-            red2.at[my_b],
-            ssem.at[SUM2],
-            rsem.at[SUM2],
-            device_id=(ctx_of(my_a, peer), ch),
-            device_id_type=MESH,
-        ).start()
-
-    red2[my_b] = red[...]
+    part2[0:2, :] = total_of(red1, group_a, SUM1)
+    exchange(
+        lambda peer: part2,
+        red2,
+        my_b,
+        group_b,
+        SUM2,
+        lambda peer: (ctx_of(my_a, peer), ch),
+        lambda: part2[...],
+    )
 
     tail.wait_recv()
     for i, ref in enumerate((gq_ref, gk_ref, gv_ref)):
@@ -330,49 +370,70 @@
             for j in range(1, 3):
                 total = total + taps_at(j, cs) * back[i, j : j + rows, cs]
             ref[:, cs] = total.astype(BF16)
-
-    wait_many(red2, group_b - 1, rsem.at[SUM2])
-    wait_many(red2, group_b - 1, ssem.at[SUM2])
-    sums = red2[0]
-    for i in range(1, group_b):
-        sums = sums + red2[i]
-    row = lax.broadcasted_iota(jnp.int32, sums.shape, 0)
-    squares = jnp.where(row < 4, sums * sums, sums)
-    nrm[...] = jnp.broadcast_to(jnp.sum(squares, keepdims=True), nrm.shape)
-
-    @pl.loop(1, chs)
-    def _(step):
-        peer = lax.rem(ch + step, chs)
-        pltpu.make_async_remote_copy(
-            nrm,
-            nrmd.at[ch],
-            ssem.at[NORM],
-            rsem.at[NORM],
-            device_id=(me, peer),
-            device_id_type=MESH,
-        ).start()
-
-    nrmd[ch] = nrm[...]
+        stores[1 + i].start()
+
+    part3[...] = total_of(red2, group_b, SUM2)
+    exchange(lambda peer: part3, red3, my_a, group_a, SUM3, along_a, lambda: part3[...])
 
     arrived(5)
     for cb, cs in enumerate(blocks):
-        gkern_ref[:, cs] = from_pieces(5, cb)
-
-    wait_many(nrmd, chs - 1, rsem.at[NORM])
-    wait_many(nrmd, chs - 1, ssem.at[NORM])
-    norm_sq = nrmd[0]
-    for i in range(1, chs):
-        norm_sq = norm_sq + nrmd[i]
-    factor = limit / jnp.maximum(jnp.sqrt(norm_sq), limit)
-    factor = factor[0:1, 0:1]
-    small_ref[...] = factor * sums
-    gkern_ref[...] = factor * gkern_ref[...]
-
+        lag_ref[:, cs] = from_pieces(5, cb).astype(BF16)
+    stores[4].start()
+
+    wait_many(red3, group_a, rsem.at[SUM3])
+    row = lax.broadcasted_iota(jnp.int32, part3.shape, 0)
+    square = jnp.zeros(part3.shape, F32)
+    for a in range(group_a):
+        piece = red3[a]
+        square = square + jnp.where(row < 2, piece * piece, piece)
+        first = 2 * (a % 2)
+        small_ref[first : first + 2, a // 2 * LANES : (a // 2 + 1) * LANES] = piece[0:2]
+    nrm[...] = jnp.broadcast_to(jnp.sum(square, keepdims=True), nrm.shape)
+    exchange(
+        lambda peer: nrm, nrmd, ch, chs, NORM, lambda peer: (me, peer), lambda: nrm[...]
+    )
+    stores[5].start()
+    norm_sq = total_of(nrmd, chs, NORM)
+    factor_ref[...] = limit / jnp.maximum(jnp.sqrt(norm_sq), limit)
+    stores[6].start()
+
+    wait_many(red1, group_a, ssem.at[SUM1])
+    wait_many(red2, group_b, ssem.at[SUM2])
+    wait_many(red3, group_a, ssem.at[SUM3])
+    wait_many(nrmd, chs, ssem.at[NORM])
     halo.wait_send()
     tail.wait_send()
     for slot in range(6):
         view = src.at[slot, pl.ds(0, pieces - 1)]
         pltpu.make_async_copy(view, view, ssem.at[KERN + slot]).wait()
+    for store in stores:
+        store.wait()
+
+
+def store_kernel(*refs):
+    parts, outs, near, refs = refs[:7], refs[7:14], refs[14:21], refs[21:]
+    kern, short, skip, isem, osem = refs
+    lag_ref, small_ref, factor_ref = near[4:]
+    loads = [pltpu.make_async_copy(a, b, isem.at[i]) for i, (a, b) in enumerate(zip(parts, near))]
+    order = (6, 4, 5, 0, 1, 2, 3)
+    for i in order:
+        loads[i].start()
+    ready = (*near[:4], kern, short, skip)
+    stores = [pltpu.make_async_copy(a, b, osem.at[i]) for i, (a, b) in enumerate(zip(ready, outs))]
+    for i in order[:3]:
+        loads[i].wait()
+    factor = factor_ref[0:1, 0:1]
+    kern[...] = factor * lag_ref[...].astype(F32)
+    stores[4].start()
+    short[...] = factor * small_ref[0:3, :]
+    skip[...] = (factor * small_ref[3:4, :]).reshape(skip.shape)
+    stores[5].start()
+    stores[6].start()
+    for i in range(4):
+        loads[i].wait()
+        stores[i].start()
+    for store in stores:
+        store.wait()
 
 
 def body(sizes, q_in, k_in, v_in, grad_out, short_filter, kernel, skip):
@@ -382,46 +443,81 @@
     limit = math.sqrt(float(pieces * rows * channels * chs))
     consts = [jnp.asarray(table) for table in tables(pieces, rows)]
     wide = jax.ShapeDtypeStruct((rows, channels), BF16)
-    vmem = pl.BlockSpec(memory_space=pltpu.VMEM)
-    mixed, grad_q, grad_k, grad_v, grad_kernel, small = pl.pallas_call(
+    far = pl.BlockSpec(memory_space=pltpu.HBM)
+    operands = [kernel, k_in, v_in, q_in, grad_out, short_filter]
+    operands += [consts[0], consts[2], consts[4], consts[5], consts[1], consts[3]]
+    operands.append(skip[None, :])
+    f32_wide = jax.ShapeDtypeStruct((rows, channels), F32)
+    results = [
+        wide,
+        wide,
+        wide,
+        wide,
+        wide,
+        jax.ShapeDtypeStruct((4, channels), F32),
+        jax.ShapeDtypeStruct((1, LANES), F32),
+    ]
+    parts = pl.pallas_call(
         functools.partial(mixer_kernel, (pieces, group_a, group_b, chs), limit),
+        out_shape=results,
+        in_specs=[far] * 13,
+        out_specs=[far] * 7,
+        scratch_shapes=[
+            *(pltpu.VMEM(x.shape, x.dtype) for x in operands),
+            *(pltpu.VMEM(x.shape, x.dtype) for x in results),
+            pltpu.VMEM((6, pieces, OWN, rows), BF16),
+            pltpu.VMEM((6, pieces, OWN, rows), BF16),
+            pltpu.VMEM((3, rows + 8, channels), F32),
+            pltpu.VMEM((5, rows, channels), F32),
+            pltpu.VMEM((3, rows + 8, channels), F32),
+            *(pltpu.VMEM((8, channels), F32) for _ in range(4)),
+            pltpu.VMEM((pieces * OWN, rows), F32),
+            pltpu.VMEM((pieces * OWN, 2 * rows), BF16),
+            pltpu.VMEM((3, pieces * OWN, 2 * rows), F32),
+            pltpu.VMEM((group_a, 2, LANES), F32),
+            pltpu.VMEM((group_a, 2, LANES), F32),
+            pltpu.VMEM((4, LANES), F32),
+            pltpu.VMEM((group_b, 4, LANES), F32),
+            pltpu.VMEM((4, LANES), F32),
+            pltpu.VMEM((group_a, 4, LANES), F32),
+            pltpu.VMEM((1, LANES), F32),
+            pltpu.VMEM((chs, 1, LANES), F32),
+            pltpu.SemaphoreType.DMA((12,)),
+            pltpu.SemaphoreType.DMA((12,)),
+            pltpu.SemaphoreType.DMA((13,)),
+            pltpu.SemaphoreType.DMA((7,)),
+        ],
+        compiler_params=pltpu.CompilerParams(
+            collective_id=0, has_side_effects=True, vmem_limit_bytes=63 << 20
+        ),
+        name="mixer",
+    )(*operands)
+    out = pl.pallas_call(
+        store_kernel,
         out_shape=[
             wide,
             wide,
             wide,
             wide,
-            jax.ShapeDtypeStruct((rows, channels), F32),
-            jax.ShapeDtypeStruct((8, channels), F32),
+            f32_wide,
+            jax.ShapeDtypeStruct((3, channels), F32),
+            jax.ShapeDtypeStruct((channels,), F32),
         ],
-        in_specs=[vmem] * 13,
-        out_specs=[vmem] * 6,
+        in_specs=[far] * 7,
+        out_specs=[far] * 7,
         scratch_shapes=[
-            pltpu.VMEM((6, pieces, OWN, rows), BF16),
-            pltpu.VMEM((6, pieces, OWN, rows), BF16),
-            pltpu.VMEM((3, rows + 8, channels), F32),
-            pltpu.VMEM((5, rows, channels), F32),
-            pltpu.VMEM((3, rows + 8, channels), F32),
-            pltpu.VMEM((8, channels), F32),
-            pltpu.VMEM((8, channels), F32),
-            pltpu.VMEM((8, channels), F32),
-            pltpu.VMEM((8, channels), F32),
-            pltpu.VMEM((pieces * OWN, rows), F32),
-            pltpu.VMEM((pieces * OWN, 2 * rows), BF16),
-            pltpu.VMEM((3, pieces * OWN, 2 * rows), F32),
-            pltpu.VMEM((8, channels), F32),
-            pltpu.VMEM((group_a, 8, channels), F32),
-            pltpu.VMEM((group_b, 8, channels), F32),
-            pltpu.VMEM((8, LANES), F32),
-            pltpu.VMEM((chs, 8, LANES), F32),
-            pltpu.SemaphoreType.DMA((11,)),
-            pltpu.SemaphoreType.DMA((11,)),
+            *(pltpu.VMEM(x.shape, x.dtype) for x in results),
+            pltpu.VMEM((rows, channels), F32),
+            pltpu.VMEM((3, channels), F32),
+            pltpu.VMEM((channels,), F32),
+            pltpu.SemaphoreType.DMA((7,)),
+            pltpu.SemaphoreType.DMA((7,)),
         ],
-        compiler_params=pltpu.CompilerParams(
-            collective_id=0, has_side_effects=True, vmem_limit_bytes=40 << 20
-        ),
-        name="mixer",
-    )(q_in, k_in, v_in, grad_out, kernel, short_filter, skip[None, :], *consts)
-    return mixed, grad_q, grad_k, grad_v, small[:3], small[3], grad_kernel
+        compiler_params=pltpu.CompilerParams(vmem_limit_bytes=63 << 20),
+        name="store",
+    )(*parts)
+    mixed, grad_q, grad_k, grad_v, grad_kernel, grad_short, grad_skip = out
+    return mixed, grad_q, grad_k, grad_v, grad_short, grad_skip, grad_kernel
 
 
 def solution(mesh):

time: 69.5 us -> 57.3 us (0.82)
  local copies, waits for them, and re-layouts: 15.3 us -> 0 us
  Pallas kernels: 52.9 us -> 56.5 us
    unnamed x31 -> x0, local copies, waits for them, and re-layouts: 14.1 us -> none
    pallas_call x0 -> x1, Pallas kernels: none -> 2 us  [body(): pl.pallas_call(store_kernel, out_shape=[wide, wide, wide, wide, f32_wide,...]
    pallas_call x1, Pallas kernels: 52.9 us -> 54.5 us  [body(): pl.pallas_call(functools.partial(mixer_kernel, (pieces, group_a, group_b,...]
    slice x2 -> x0, local copies, waits for them, and re-layouts: 1.18 us -> none  [body(): return (mixed, grad_q, grad_k, grad_v, small[:3], small[3], grad_kernel)]
where the time goes in v2:
time: 57.3 us; the launch traced here: 57.2 us
  Pallas kernels  56.5 us (99%)
  between operations  0.64 us (1%)
    pallas_call x1, Pallas kernels, body(): pl.pallas_call(functools.partial(mixer_kernel, (pieces, group_a, group_b,...  54.5 us
    pallas_call x1, Pallas kernels, body(): pl.pallas_call(store_kernel, out_shape=[wide, wide, wide, wide, f32_wide,...  2 us

profile of v2, /device:TPU:1, one launch (start us, length us, event | category | flops | bytes accessed | tf_op | source)
XLA Modules:
  0.0 57.2 jit_solution(10760634654582882615)
XLA Ops:
  0.6 54.5 %mixer.1 = (bf16[128,512]{1,0:T(8,128)(2,1)}, bf16[128,512]{1,0:T(8,128)(2,1)}, bf16[128,512]{1,0:T(8,128)(2,1)}, bf16[128,512]{1,0:T(8,128)(2,1)}, bf16[128,512...) custom-call(f32[128,512]{1,0:T(8,128)} %refs_0_.1, bf16[128,512]{1,0:T(8,128)(2,1)} %refs_1_.1, ...), custom_call_target="tpu_custom_call" | custom-call | tf_op jit(solution)/shard_map/mixer/pallas_call | solution.py:460
  55.2 2.0 %store.1 = (bf16[128,512]{1,0:T(8,128)(2,1)}, bf16[128,512]{1,0:T(8,128)(2,1)}, bf16[128,512]{1,0:T(8,128)(2,1)}, bf16[128,512]{1,0:T(8,128)(2,1)}, f32[128,512]...) custom-call(bf16[128,512]{1,0:T(8,128)(2,1)} %get-tuple-element.21.refs_0_, bf16[128,512]{1,0:T(8,128)(2,1)} %get-tuple-element.22.refs_1_, ...), custom_call_target="tpu_custom_call" | custom-call | tf_op jit(solution)/shard_map/store/pallas_call | solution.py:495

commit v3 on v2

--- a/solution.py
+++ b/solution.py
@@ -14,7 +14,7 @@
 BF16 = jnp.bfloat16
 LANES = 128
 OWN = 8
-HALO, KERN, PROD, BACK, CONV, CORR, LAG, TAIL, SUM1, SUM2, SUM3, NORM = range(12)
+HALO, KERN, PROD, BACK, CONV, CORR, LAG, TAIL, SUM1, SUM2, NORM = range(11)
 
 
 def split_table(table):
@@ -41,6 +41,10 @@
         np.cos(twist).astype(np.float32),
         np.sin(twist).astype(np.float32),
     )
+
+
+def by_distance(size):
+    return sorted(range(size), key=lambda k: -min(k, size - k))
 
 
 def mixer_kernel(
@@ -66,7 +70,6 @@
     ini_ref,
     skip_ref,
     ) = loaded
-    ready, refs = refs[:7], refs[7:]
     (
     mixed_ref,
     gq_ref,
@@ -75,7 +78,7 @@
     lag_ref,
     small_ref,
     factor_ref,
-    ) = ready
+    ) = outputs
     (
     src,
     dst,
@@ -89,18 +92,14 @@
     tmp,
     bbuf,
     spec,
-    part1,
+    part,
     red1,
-    part2,
     red2,
-    part3,
-    red3,
     nrm,
     nrmd,
     ssem,
     rsem,
     isem,
-    osem,
     ) = refs
     pieces, group_a, group_b, chs = dims
     rows, channels = q_ref.shape
@@ -112,6 +111,30 @@
     def ctx_of(a, b):
         return (a // 2 * group_b + b) * 2 + a % 2
 
+    others = [k for k in by_distance(group_a) if k]
+    corners = {k: ctx_of(lax.rem(my_a + k, group_a), 0) for k in range(group_a)}
+
+    def each_peer(visit):
+        @pl.loop(0, group_b - 1)
+        def _(i):
+            ahead = i // 2 * (1 - i % 2) - (i + 1) // 2 * (i % 2)
+            b = lax.rem(my_b + group_b // 2 + ahead, group_b)
+            for k in by_distance(group_a):
+                visit(corners[k] + 2 * b)
+
+        for k in others:
+            visit(corners[k] + 2 * my_b)
+
+    barrier = pltpu.get_barrier_semaphore()
+
+    def greet(a, b):
+        pl.semaphore_signal(barrier, inc=1, device_id=(a, b), device_id_type=MESH)
+
+    each_peer(lambda peer: greet(peer, ch))
+    for k in by_distance(chs):
+        if k:
+            greet(me, lax.rem(ch + k, chs))
+
     loads = [
         pltpu.make_async_copy(far, near, isem.at[i])
         for i, (far, near) in enumerate(zip(inputs, loaded))
@@ -119,22 +142,8 @@
     for load in loads:
         load.start()
 
-    barrier = pltpu.get_barrier_semaphore()
-
-    @pl.loop(1, pieces, unroll=9)
-    def _(step):
-        peer = lax.rem(me + step, pieces)
-        pl.semaphore_signal(barrier, inc=1, device_id=(peer, ch), device_id_type=MESH)
-
-    @pl.loop(1, chs)
-    def _(step):
-        peer = lax.rem(ch + step, chs)
-        pl.semaphore_signal(barrier, inc=1, device_id=(me, peer), device_id_type=MESH)
-
     def spread(slot):
-        @pl.loop(1, pieces, unroll=9)
-        def _(step):
-            peer = lax.rem(me + step, pieces)
+        def send(peer):
             pltpu.make_async_remote_copy(
                 src.at[slot, peer],
                 dst.at[slot, me],
@@ -144,6 +153,7 @@
                 device_id_type=MESH,
             ).start()
 
+        each_peer(send)
         dst[slot, me] = src[slot, me]
 
     def arrived(slot):
@@ -160,11 +170,6 @@
         return block.reshape(LANES, rows).T
 
     blocks = [slice(cb * LANES, (cb + 1) * LANES) for cb in range(channels // LANES)]
-
-    stores = [
-        pltpu.make_async_copy(near, far, osem.at[i])
-        for i, (near, far) in enumerate(zip(ready, outputs))
-    ]
 
     loads[0].wait()
     for cb, cs in enumerate(blocks):
@@ -217,7 +222,7 @@
         back_mix = go_ref[:, cs].astype(F32) * q_short
         wide[0, :, cs] = q_short
         wide[4, :, cs] = back_mix
-        part1[2 * cb + 1, 1:2, :] = jnp.sum(back_mix * wide[3, :, cs], axis=0, keepdims=True)
+        part[3:4, cs] = jnp.sum(back_mix * wide[3, :, cs], axis=0, keepdims=True)
         to_pieces(2, cb, back_mix)
     spread(2)
 
@@ -281,15 +286,14 @@
     square = inverse(5, 1, 2, True)
     spread(5)
 
-    part2[2:3, :] = square
-    part2[3:4, :] = jnp.zeros_like(square)
+    part[:, channels:] = jnp.zeros((4, LANES), F32)
+    part[0:1, channels:] = square
 
     arrived(3)
     for cb, cs in enumerate(blocks):
         filtered = from_pieces(3, cb) + skip_ref[:, cs] * wide[3, :, cs]
         mixed_ref[:, cs] = (wide[0, :, cs] * filtered).astype(BF16)
         back[0, :rows, cs] = go_ref[:, cs].astype(F32) * filtered
-    stores[0].start()
     arrived(4)
     for cb, cs in enumerate(blocks):
         back_prod = from_pieces(4, cb) + skip_ref[:, cs] * wide[4, :, cs]
@@ -299,23 +303,20 @@
             total = back[0, :rows, cs] * ext[0, 8 - j : 8 - j + rows, cs]
             for i in range(1, 3):
                 total = total + back[i, :rows, cs] * ext[i, 8 - j : 8 - j + rows, cs]
-            here = 2 * cb + j // 2
-            part1[here, j % 2 : j % 2 + 1, :] = jnp.sum(total, axis=0, keepdims=True)
-
-    def exchange(source, slots, mine, size, sem, device_of, own):
-        @pl.loop(1, size, unroll=True)
-        def _(step):
-            peer = lax.rem(mine + step, size)
-            pltpu.make_async_remote_copy(
-                source(peer),
-                slots.at[mine],
-                ssem.at[sem],
-                rsem.at[sem],
-                device_id=device_of(peer),
-                device_id_type=MESH,
-            ).start()
-
-        slots[mine] = own()
+            part[j : j + 1, cs] = jnp.sum(total, axis=0, keepdims=True)
+
+    def exchange(source, slots, mine, size, sem, device_of):
+        for k in by_distance(size):
+            if k:
+                pltpu.make_async_remote_copy(
+                    source,
+                    slots.at[mine],
+                    ssem.at[sem],
+                    rsem.at[sem],
+                    device_id=device_of(lax.rem(mine + k, size)),
+                    device_id_type=MESH,
+                ).start()
+        slots[mine] = source[...]
 
     def wait_many(slots, size, sem):
         view = slots.at[pl.ds(0, size - 1)]
@@ -328,12 +329,7 @@
             total = total + slots[i]
         return total
 
-    def along_a(peer):
-        return (ctx_of(peer, my_b), ch)
-
-    exchange(
-        lambda peer: part1.at[peer], red1, my_a, group_a, SUM1, along_a, lambda: part1[my_a]
-    )
+    exchange(part, red1, my_a, group_a, SUM1, lambda peer: (ctx_of(peer, my_b), ch))
 
     for i in range(3):
         tsrc[2 * i : 2 * i + 2, :] = back[i, 0:2, :]
@@ -348,16 +344,10 @@
     )
     tail.start()
 
-    part2[0:2, :] = total_of(red1, group_a, SUM1)
-    exchange(
-        lambda peer: part2,
-        red2,
-        my_b,
-        group_b,
-        SUM2,
-        lambda peer: (ctx_of(my_a, peer), ch),
-        lambda: part2[...],
-    )
+    sums = total_of(red1, group_a, SUM1)
+    wait_many(red1, group_a, ssem.at[SUM1])
+    part[...] = sums
+    exchange(part, red2, my_b, group_b, SUM2, lambda peer: (ctx_of(my_a, peer), ch))
 
     tail.wait_recv()
     for i, ref in enumerate((gq_ref, gk_ref, gv_ref)):
@@ -370,70 +360,50 @@
             for j in range(1, 3):
                 total = total + taps_at(j, cs) * back[i, j : j + rows, cs]
             ref[:, cs] = total.astype(BF16)
-        stores[1 + i].start()
-
-    part3[...] = total_of(red2, group_b, SUM2)
-    exchange(lambda peer: part3, red3, my_a, group_a, SUM3, along_a, lambda: part3[...])
+
+    sums = total_of(red2, group_b, SUM2)
+    squares = sums[:, :channels] * sums[:, :channels]
+    square = jnp.sum(squares, keepdims=True) + jnp.sum(sums[:, channels:], keepdims=True)
+    nrm[...] = jnp.broadcast_to(square, nrm.shape)
+    exchange(nrm, nrmd, ch, chs, NORM, lambda peer: (me, peer))
+    small_ref[...] = sums[:, :channels]
 
     arrived(5)
     for cb, cs in enumerate(blocks):
-        lag_ref[:, cs] = from_pieces(5, cb).astype(BF16)
-    stores[4].start()
-
-    wait_many(red3, group_a, rsem.at[SUM3])
-    row = lax.broadcasted_iota(jnp.int32, part3.shape, 0)
-    square = jnp.zeros(part3.shape, F32)
-    for a in range(group_a):
-        piece = red3[a]
-        square = square + jnp.where(row < 2, piece * piece, piece)
-        first = 2 * (a % 2)
-        small_ref[first : first + 2, a // 2 * LANES : (a // 2 + 1) * LANES] = piece[0:2]
-    nrm[...] = jnp.broadcast_to(jnp.sum(square, keepdims=True), nrm.shape)
-    exchange(
-        lambda peer: nrm, nrmd, ch, chs, NORM, lambda peer: (me, peer), lambda: nrm[...]
-    )
-    stores[5].start()
+        lag_ref[:, cs] = from_pieces(5, cb)
+
     norm_sq = total_of(nrmd, chs, NORM)
     factor_ref[...] = limit / jnp.maximum(jnp.sqrt(norm_sq), limit)
-    stores[6].start()
-
-    wait_many(red1, group_a, ssem.at[SUM1])
+
     wait_many(red2, group_b, ssem.at[SUM2])
-    wait_many(red3, group_a, ssem.at[SUM3])
     wait_many(nrmd, chs, ssem.at[NORM])
     halo.wait_send()
     tail.wait_send()
     for slot in range(6):
         view = src.at[slot, pl.ds(0, pieces - 1)]
         pltpu.make_async_copy(view, view, ssem.at[KERN + slot]).wait()
-    for store in stores:
-        store.wait()
 
 
 def store_kernel(*refs):
-    parts, outs, near, refs = refs[:7], refs[7:14], refs[14:21], refs[21:]
-    kern, short, skip, isem, osem = refs
+    near, far, (kern, short, skip, sem) = refs[:7], refs[7:14], refs[14:]
     lag_ref, small_ref, factor_ref = near[4:]
-    loads = [pltpu.make_async_copy(a, b, isem.at[i]) for i, (a, b) in enumerate(zip(parts, near))]
-    order = (6, 4, 5, 0, 1, 2, 3)
-    for i in order:
-        loads[i].start()
-    ready = (*near[:4], kern, short, skip)
-    stores = [pltpu.make_async_copy(a, b, osem.at[i]) for i, (a, b) in enumerate(zip(ready, outs))]
-    for i in order[:3]:
-        loads[i].wait()
+    copies = [pltpu.make_async_copy(a, b, sem.at[i]) for i, (a, b) in enumerate(zip(near[:4], far))]
+    for copy in copies:
+        copy.start()
     factor = factor_ref[0:1, 0:1]
-    kern[...] = factor * lag_ref[...].astype(F32)
-    stores[4].start()
+    step = kern.shape[0] // 4
+    for i in range(4):
+        here = pl.ds(i * step, step)
+        kern[here, :] = factor * lag_ref[here, :]
+        copies.append(pltpu.make_async_copy(kern.at[here], far[4].at[here], sem.at[4 + i]))
+        copies[-1].start()
     short[...] = factor * small_ref[0:3, :]
     skip[...] = (factor * small_ref[3:4, :]).reshape(skip.shape)
-    stores[5].start()
-    stores[6].start()
-    for i in range(4):
-        loads[i].wait()
-        stores[i].start()
-    for store in stores:
-        store.wait()
+    for i, (a, b) in enumerate(((short, far[5]), (skip, far[6]))):
+        copies.append(pltpu.make_async_copy(a, b, sem.at[8 + i]))
+        copies[-1].start()
+    for copy in copies:
+        copy.wait()
 
 
 def body(sizes, q_in, k_in, v_in, grad_out, short_filter, kernel, skip):
@@ -444,6 +414,7 @@
     consts = [jnp.asarray(table) for table in tables(pieces, rows)]
     wide = jax.ShapeDtypeStruct((rows, channels), BF16)
     far = pl.BlockSpec(memory_space=pltpu.HBM)
+    near = pl.BlockSpec(memory_space=pltpu.VMEM)
     operands = [kernel, k_in, v_in, q_in, grad_out, short_filter]
     operands += [consts[0], consts[2], consts[4], consts[5], consts[1], consts[3]]
     operands.append(skip[None, :])
@@ -453,7 +424,7 @@
         wide,
         wide,
         wide,
-        wide,
+        f32_wide,
         jax.ShapeDtypeStruct((4, channels), F32),
         jax.ShapeDtypeStruct((1, LANES), F32),
     ]
@@ -461,10 +432,9 @@
         functools.partial(mixer_kernel, (pieces, group_a, group_b, chs), limit),
         out_shape=results,
         in_specs=[far] * 13,
-        out_specs=[far] * 7,
+        out_specs=[near] * 7,
         scratch_shapes=[
             *(pltpu.VMEM(x.shape, x.dtype) for x in operands),
-            *(pltpu.VMEM(x.shape, x.dtype) for x in results),
             pltpu.VMEM((6, pieces, OWN, rows), BF16),
             pltpu.VMEM((6, pieces, OWN, rows), BF16),
             pltpu.VMEM((3, rows + 8, channels), F32),
@@ -474,24 +444,20 @@
             pltpu.VMEM((pieces * OWN, rows), F32),
             pltpu.VMEM((pieces * OWN, 2 * rows), BF16),
             pltpu.VMEM((3, pieces * OWN, 2 * rows), F32),
-            pltpu.VMEM((group_a, 2, LANES), F32),
-            pltpu.VMEM((group_a, 2, LANES), F32),
-            pltpu.VMEM((4, LANES), F32),
-            pltpu.VMEM((group_b, 4, LANES), F32),
-            pltpu.VMEM((4, LANES), F32),
-            pltpu.VMEM((group_a, 4, LANES), F32),
+            pltpu.VMEM((4, channels + LANES), F32),
+            pltpu.VMEM((group_a, 4, channels + LANES), F32),
+            pltpu.VMEM((group_b, 4, channels + LANES), F32),
             pltpu.VMEM((1, LANES), F32),
             pltpu.VMEM((chs, 1, LANES), F32),
-            pltpu.SemaphoreType.DMA((12,)),
-            pltpu.SemaphoreType.DMA((12,)),
+            pltpu.SemaphoreType.DMA((11,)),
+            pltpu.SemaphoreType.DMA((11,)),
             pltpu.SemaphoreType.DMA((13,)),
-            pltpu.SemaphoreType.DMA((7,)),
         ],
         compiler_params=pltpu.CompilerParams(
-            collective_id=0, has_side_effects=True, vmem_limit_bytes=63 << 20
+            collective_id=0, has_side_effects=True, vmem_limit_bytes=40 << 20
         ),
         name="mixer",
-    )(*operands)
+    )(*[pltpu.with_memory_space_constraint(x, pltpu.HBM) for x in operands])
     out = pl.pallas_call(
         store_kernel,
         out_shape=[
@@ -503,17 +469,15 @@
             jax.ShapeDtypeStruct((3, channels), F32),
             jax.ShapeDtypeStruct((channels,), F32),
         ],
-        in_specs=[far] * 7,
+        in_specs=[near] * 7,
         out_specs=[far] * 7,
         scratch_shapes=[
-            *(pltpu.VMEM(x.shape, x.dtype) for x in results),
             pltpu.VMEM((rows, channels), F32),
             pltpu.VMEM((3, channels), F32),
             pltpu.VMEM((channels,), F32),
-            pltpu.SemaphoreType.DMA((7,)),
-            pltpu.SemaphoreType.DMA((7,)),
+            pltpu.SemaphoreType.DMA((10,)),
         ],
-        compiler_params=pltpu.CompilerParams(vmem_limit_bytes=63 << 20),
+        compiler_params=pltpu.CompilerParams(vmem_limit_bytes=16 << 20),
         name="store",
     )(*parts)
     mixed, grad_q, grad_k, grad_v, grad_kernel, grad_short, grad_skip = out

time: 57.3 us -> 50.8 us (0.89)
  Pallas kernels: 56.5 us -> 50.1 us
    pallas_call x1, Pallas kernels: 54.5 us -> 49.1 us  [body(): pl.pallas_call(functools.partial(mixer_kernel, (pieces, group_a, group_b,...]
    pallas_call x1, Pallas kernels: 2 us -> 0.96 us  [body(): pl.pallas_call(store_kernel, out_shape=[wide, wide, wide, wide, f32_wide,...]
where the time goes in v3:
time: 50.8 us; the launch traced here: 50.7 us
  Pallas kernels  50.1 us (99%)
  between operations  0.64 us (1%)
    pallas_call x1, Pallas kernels, body(): pl.pallas_call(functools.partial(mixer_kernel, (pieces, group_a, group_b,...  49.1 us

profile of v3, /device:TPU:1, one launch (start us, length us, event | category | flops | bytes accessed | tf_op | source)
XLA Modules:
  0.0 50.7 jit_solution(15054857626145689632)
XLA Ops:
  0.6 49.1 %mixer.1 = (bf16[128,512]{1,0:T(8,128)(2,1)S(1)}, bf16[128,512]{1,0:T(8,128)(2,1)S(1)}, bf16[128,512]{1,0:T(8,128)(2,1)S(1)}, bf16[128,512]{1,0:T(8,128)(2,1)S(1...) custom-call(f32[128,512]{1,0:T(8,128)} %refs_0_.1, bf16[128,512]{1,0:T(8,128)(2,1)} %refs_1_.1, ...), custom_call_target="tpu_custom_call" | custom-call | tf_op jit(solution)/shard_map/mixer/pallas_call | solution.py:431
  49.7 1.0 %store.1 = (bf16[128,512]{1,0:T(8,128)(2,1)}, bf16[128,512]{1,0:T(8,128)(2,1)}, bf16[128,512]{1,0:T(8,128)(2,1)}, bf16[128,512]{1,0:T(8,128)(2,1)}, f32[128,512]...) custom-call(bf16[128,512]{1,0:T(8,128)(2,1)S(1)} %get-tuple-element.21.refs_0_, ...), custom_call_target="tpu_custom_call" | custom-call | tf_op jit(solution)/shard_map/store/pallas_call | solution.py:461

commit v4 on v3

--- a/solution.py
+++ b/solution.py
@@ -36,8 +36,8 @@
     return (
         np.concatenate(split_table(out_f), axis=1),
         np.concatenate(split_table(out_i), axis=1),
-        split_table(in_f)[0],
-        split_table(in_i)[0],
+        *split_table(in_f),
+        *split_table(in_i),
         np.cos(twist).astype(np.float32),
         np.sin(twist).astype(np.float32),
     )
@@ -52,9 +52,9 @@
     limit,
     *refs,
 ):
-    inputs, refs = refs[:13], refs[13:]
+    inputs, refs = refs[:15], refs[15:]
     outputs, refs = refs[:7], refs[7:]
-    loaded, refs = refs[:13], refs[13:]
+    loaded, refs = refs[:15], refs[15:]
     (
     kern_ref,
     k_ref,
@@ -64,10 +64,12 @@
     taps_ref,
     outf_ref,
     inf_ref,
+    inf_low_ref,
     tcos_ref,
     tsin_ref,
     outi_ref,
     ini_ref,
+    ini_low_ref,
     skip_ref,
     ) = loaded
     (
@@ -83,6 +85,8 @@
     src,
     dst,
     ext,
+    go_wide,
+    corr,
     wide,
     back,
     hsrc,
@@ -91,8 +95,11 @@
     tdst,
     tmp,
     bbuf,
+    blow,
     spec,
+    weight,
     part,
+    part2,
     red1,
     red2,
     nrm,
@@ -176,8 +183,7 @@
         to_pieces(0, cb, kern_ref[:, cs])
     for i, (ref, order) in enumerate(((q_ref, 3), (k_ref, 1), (v_ref, 2))):
         loads[order].wait()
-        ext[i, 8 : 8 + rows, :] = ref[...].astype(F32)
-        hsrc[2 * i : 2 * i + 2, :] = ext[i, 6 + rows : 8 + rows, :]
+        hsrc[2 * i : 2 * i + 2, :] = ref[rows - 16 :, :].astype(F32)[14:16]
     hsrc[6:8, :] = jnp.zeros((2, channels), F32)
 
     pl.semaphore_wait(barrier, pieces - 1 + chs - 1)
@@ -192,118 +198,149 @@
     )
     halo.start()
     spread(0)
+    ext[:, 0:8, :] = jnp.zeros((3, 8, channels), F32)
+    for i, ref in enumerate((q_ref, k_ref, v_ref)):
+        ext[i, 8 : 8 + rows, :] = ref[...].astype(F32)
     for load in loads[4:]:
         load.wait()
+
+    def short(i, first, count, cs):
+        total = taps_ref[0:1, cs] * ext[i, 8 + first : 8 + first + count, cs]
+        for j in range(1, 3):
+            start = 8 - j + first
+            total = total + taps_ref[j : j + 1, cs] * ext[i, start : start + count, cs]
+        return total
+
+    def local_part(first, count, cs):
+        here = slice(first, first + count)
+        q_short, k_short, v_short = (short(i, first, count, cs) for i in range(3))
+        wide[0, here, cs] = q_short
+        wide[1, here, cs] = k_short
+        wide[2, here, cs] = v_short
+        wide[3, here, cs] = (k_short * v_short).astype(BF16).astype(F32)
+        wide[4, here, cs] = go_wide[here, cs] * q_short
+
+    go_wide[...] = go_ref[...].astype(F32)
+    for cs in blocks:
+        local_part(0, rows, cs)
     halo.wait_recv()
-
-    def taps_at(j, cs):
-        return taps_ref[j : j + 1, cs]
-
-    def short(i, cs):
-        total = taps_at(0, cs) * ext[i, 8 : 8 + rows, cs]
-        for j in range(1, 3):
-            total = total + taps_at(j, cs) * ext[i, 8 - j : 8 - j + rows, cs]
-        return total
-
     for i in range(3):
         halo_rows = hdst[2 * i : 2 * i + 2, :]
         ext[i, 6:8, :] = jnp.where(me > 0, halo_rows, jnp.zeros_like(halo_rows))
+    for cs in blocks:
+        local_part(0, 8, cs)
     for cb, cs in enumerate(blocks):
-        k_short = short(1, cs)
-        v_short = short(2, cs)
-        product = (k_short * v_short).astype(BF16).astype(F32)
-        wide[1, :, cs] = k_short
-        wide[2, :, cs] = v_short
-        wide[3, :, cs] = product
-        to_pieces(1, cb, product)
+        to_pieces(1, cb, wide[3, :, cs])
     spread(1)
     for cb, cs in enumerate(blocks):
-        q_short = short(0, cs)
-        back_mix = go_ref[:, cs].astype(F32) * q_short
-        wide[0, :, cs] = q_short
-        wide[4, :, cs] = back_mix
+        to_pieces(2, cb, wide[4, :, cs])
+    spread(2)
+
+    for cs in blocks:
+        back_mix = wide[4, :, cs]
         part[3:4, cs] = jnp.sum(back_mix * wide[3, :, cs], axis=0, keepdims=True)
-        to_pieces(2, cb, back_mix)
-    spread(2)
-
-    def transform(slot):
+        for j in range(3):
+            here = slice(8 - j, 8 - j + rows)
+            pair = wide[2, :, cs] * ext[1, here, cs] + wide[1, :, cs] * ext[2, here, cs]
+            weight[j, :, cs] = pair
+            part[j : j + 1, cs] = skip_ref[:, cs] * jnp.sum(
+                back_mix * pair, axis=0, keepdims=True
+            )
+
+    def put(here, columns, value, precise):
+        high = value.astype(BF16)
+        bbuf[here, columns] = high
+        if precise:
+            blow[here, columns] = (value - high.astype(F32)).astype(BF16)
+
+    def inner(high, low, precise):
+        total = jnp.dot(bbuf[...], high[...], preferred_element_type=F32)
+        if precise:
+            total = total + jnp.dot(bbuf[...], low[...], preferred_element_type=F32)
+            total = total + jnp.dot(blow[...], high[...], preferred_element_type=F32)
+        return total
+
+    left_half, right_half = slice(0, rows), slice(rows, 2 * rows)
+
+    def transform(slot, precise):
         tmp[...] = dst[slot].astype(F32).reshape(pieces * OWN, rows)
         cols = [tmp[pl.ds(c, pieces, stride=OWN), :] for c in range(OWN)]
         signal = jnp.concatenate(cols, axis=1).astype(BF16)
-        part = jnp.dot(
+        outer = jnp.dot(
             outf_ref[...],
             jnp.concatenate([signal, signal], axis=0),
             preferred_element_type=F32,
         )
         cos, sin = tcos_ref[...], tsin_ref[...]
         for c in range(OWN):
-            re = part[:pieces, c * rows : (c + 1) * rows]
-            im = part[pieces:, c * rows : (c + 1) * rows]
+            re = outer[:pieces, c * rows : (c + 1) * rows]
+            im = outer[pieces:, c * rows : (c + 1) * rows]
             here = slice(c * pieces, (c + 1) * pieces)
-            bbuf[here, :rows] = (re * cos + im * sin).astype(BF16)
-            bbuf[here, rows:] = (im * cos - re * sin).astype(BF16)
-        spec[slot] = jnp.dot(bbuf[...], inf_ref[...], preferred_element_type=F32)
-
-    def inverse(slot, left, right, conj):
+            put(here, left_half, re * cos + im * sin, precise)
+            put(here, right_half, im * cos - re * sin, precise)
+        spec[slot] = inner(inf_ref, inf_low_ref, precise)
+
+    def inverse(slot, left, right, conj, precise):
         a_re, a_im = spec[left, :, :rows], spec[left, :, rows:]
         b_re, b_im = spec[right, :, :rows], spec[right, :, rows:]
         if conj:
-            bbuf[:, :rows] = (a_re * b_re + a_im * b_im).astype(BF16)
-            bbuf[:, rows:] = (a_re * b_im - a_im * b_re).astype(BF16)
-        else:
-            bbuf[:, :rows] = (a_re * b_re - a_im * b_im).astype(BF16)
-            bbuf[:, rows:] = (a_re * b_im + a_im * b_re).astype(BF16)
-        part = jnp.dot(bbuf[...], ini_ref[...], preferred_element_type=F32)
+            a_im = -a_im
+        put(slice(None), left_half, a_re * b_re - a_im * b_im, precise)
+        put(slice(None), right_half, a_re * b_im + a_im * b_re, precise)
+        turned = inner(ini_ref, ini_low_ref, precise)
         cos, sin = tcos_ref[...], tsin_ref[...]
         cols = []
         for c in range(OWN):
-            re = part[c * pieces : (c + 1) * pieces, :rows]
-            im = part[c * pieces : (c + 1) * pieces, rows:]
-            turned = [(re * cos - im * sin).astype(BF16), (im * cos + re * sin).astype(BF16)]
-            cols.append(jnp.concatenate(turned, axis=0))
+            re = turned[c * pieces : (c + 1) * pieces, :rows]
+            im = turned[c * pieces : (c + 1) * pieces, rows:]
+            cols.append(jnp.concatenate([re * cos - im * sin, im * cos + re * sin], axis=0))
         turned = jnp.concatenate(cols, axis=1)
+        high = turned.astype(BF16)
         out = jnp.dot(
             outi_ref[...],
-            jnp.concatenate([turned, turned], axis=0),
+            jnp.concatenate([high, high], axis=0),
             preferred_element_type=F32,
         )
-        square = jnp.sum(out * out, axis=0, keepdims=True)
+        if precise:
+            low = (turned - high.astype(F32)).astype(BF16)
+            out = out + jnp.dot(outi_ref[:, : 2 * pieces], low, preferred_element_type=F32)
         for c in range(OWN):
             tmp[pl.ds(c, pieces, stride=OWN), :] = out[:, c * rows : (c + 1) * rows]
         src[slot] = tmp[...].reshape(pieces, OWN, rows).astype(BF16)
-        return sum(square[:, c * rows : (c + 1) * rows] for c in range(OWN))
+        return out
 
     arrived(0)
-    transform(0)
+    transform(0, True)
     arrived(1)
-    transform(1)
-    inverse(3, 0, 1, False)
+    transform(1, False)
+    inverse(3, 0, 1, False, False)
     spread(3)
     arrived(2)
-    transform(2)
-    inverse(4, 0, 2, True)
+    transform(2, False)
+    inverse(4, 0, 2, True, False)
     spread(4)
-    square = inverse(5, 1, 2, True)
+    lag = inverse(5, 1, 2, True, True)
     spread(5)
-
+    square = jnp.sum(lag * lag, axis=0, keepdims=True)
     part[:, channels:] = jnp.zeros((4, LANES), F32)
-    part[0:1, channels:] = square
+    part[0:1, channels:] = sum(square[:, c * rows : (c + 1) * rows] for c in range(OWN))
 
     arrived(3)
     for cb, cs in enumerate(blocks):
         filtered = from_pieces(3, cb) + skip_ref[:, cs] * wide[3, :, cs]
         mixed_ref[:, cs] = (wide[0, :, cs] * filtered).astype(BF16)
-        back[0, :rows, cs] = go_ref[:, cs].astype(F32) * filtered
+        back_q = go_wide[:, cs] * filtered
+        back[0, :rows, cs] = back_q
+        for j in range(3):
+            part[j : j + 1, cs] += jnp.sum(
+                back_q * ext[0, 8 - j : 8 - j + rows, cs], axis=0, keepdims=True
+            )
     arrived(4)
     for cb, cs in enumerate(blocks):
-        back_prod = from_pieces(4, cb) + skip_ref[:, cs] * wide[4, :, cs]
-        back[1, :rows, cs] = back_prod * wide[2, :, cs]
-        back[2, :rows, cs] = back_prod * wide[1, :, cs]
+        block = from_pieces(4, cb)
+        corr[:, cs] = block
         for j in range(3):
-            total = back[0, :rows, cs] * ext[0, 8 - j : 8 - j + rows, cs]
-            for i in range(1, 3):
-                total = total + back[i, :rows, cs] * ext[i, 8 - j : 8 - j + rows, cs]
-            part[j : j + 1, cs] = jnp.sum(total, axis=0, keepdims=True)
+            part[j : j + 1, cs] += jnp.sum(block * weight[j, :, cs], axis=0, keepdims=True)
 
     def exchange(source, slots, mine, size, sem, device_of):
         for k in by_distance(size):
@@ -330,6 +367,10 @@
         return total
 
     exchange(part, red1, my_a, group_a, SUM1, lambda peer: (ctx_of(peer, my_b), ch))
+    for cs in blocks:
+        back_prod = corr[:, cs] + skip_ref[:, cs] * wide[4, :, cs]
+        back[1, :rows, cs] = back_prod * wide[2, :, cs]
+        back[2, :rows, cs] = back_prod * wide[1, :, cs]
 
     for i in range(3):
         tsrc[2 * i : 2 * i + 2, :] = back[i, 0:2, :]
@@ -345,9 +386,8 @@
     tail.start()
 
     sums = total_of(red1, group_a, SUM1)
-    wait_many(red1, group_a, ssem.at[SUM1])
-    part[...] = sums
-    exchange(part, red2, my_b, group_b, SUM2, lambda peer: (ctx_of(my_a, peer), ch))
+    part2[...] = sums
+    exchange(part2, red2, my_b, group_b, SUM2, lambda peer: (ctx_of(my_a, peer), ch))
 
     tail.wait_recv()
     for i, ref in enumerate((gq_ref, gk_ref, gv_ref)):
@@ -356,9 +396,9 @@
             me < pieces - 1, tail_rows, jnp.zeros_like(tail_rows)
         )
         for cs in blocks:
-            total = taps_at(0, cs) * back[i, 0:rows, cs]
+            total = taps_ref[0:1, cs] * back[i, 0:rows, cs]
             for j in range(1, 3):
-                total = total + taps_at(j, cs) * back[i, j : j + rows, cs]
+                total = total + taps_ref[j : j + 1, cs] * back[i, j : j + rows, cs]
             ref[:, cs] = total.astype(BF16)
 
     sums = total_of(red2, group_b, SUM2)
@@ -375,6 +415,7 @@
     norm_sq = total_of(nrmd, chs, NORM)
     factor_ref[...] = limit / jnp.maximum(jnp.sqrt(norm_sq), limit)
 
+    wait_many(red1, group_a, ssem.at[SUM1])
     wait_many(red2, group_b, ssem.at[SUM2])
     wait_many(nrmd, chs, ssem.at[NORM])
     halo.wait_send()
@@ -416,7 +457,7 @@
     far = pl.BlockSpec(memory_space=pltpu.HBM)
     near = pl.BlockSpec(memory_space=pltpu.VMEM)
     operands = [kernel, k_in, v_in, q_in, grad_out, short_filter]
-    operands += [consts[0], consts[2], consts[4], consts[5], consts[1], consts[3]]
+    operands += [consts[i] for i in (0, 2, 3, 6, 7, 1, 4, 5)]
     operands.append(skip[None, :])
     f32_wide = jax.ShapeDtypeStruct((rows, channels), F32)
     results = [
@@ -431,19 +472,24 @@
     parts = pl.pallas_call(
         functools.partial(mixer_kernel, (pieces, group_a, group_b, chs), limit),
         out_shape=results,
-        in_specs=[far] * 13,
+        in_specs=[far] * 15,
         out_specs=[near] * 7,
         scratch_shapes=[
             *(pltpu.VMEM(x.shape, x.dtype) for x in operands),
             pltpu.VMEM((6, pieces, OWN, rows), BF16),
             pltpu.VMEM((6, pieces, OWN, rows), BF16),
             pltpu.VMEM((3, rows + 8, channels), F32),
+            pltpu.VMEM((rows, channels), F32),
+            pltpu.VMEM((rows, channels), F32),
             pltpu.VMEM((5, rows, channels), F32),
             pltpu.VMEM((3, rows + 8, channels), F32),
             *(pltpu.VMEM((8, channels), F32) for _ in range(4)),
             pltpu.VMEM((pieces * OWN, rows), F32),
             pltpu.VMEM((pieces * OWN, 2 * rows), BF16),
+            pltpu.VMEM((pieces * OWN, 2 * rows), BF16),
             pltpu.VMEM((3, pieces * OWN, 2 * rows), F32),
+            pltpu.VMEM((3, rows, channels), F32),
+            pltpu.VMEM((4, channels + LANES), F32),
             pltpu.VMEM((4, channels + LANES), F32),
             pltpu.VMEM((group_a, 4, channels + LANES), F32),
             pltpu.VMEM((group_b, 4, channels + LANES), F32),
@@ -451,7 +497,7 @@
             pltpu.VMEM((chs, 1, LANES), F32),
             pltpu.SemaphoreType.DMA((11,)),
             pltpu.SemaphoreType.DMA((11,)),
-            pltpu.SemaphoreType.DMA((13,)),
+            pltpu.SemaphoreType.DMA((15,)),
         ],
         compiler_params=pltpu.CompilerParams(
             collective_id=0, has_side_effects=True, vmem_limit_bytes=40 << 20

time: 50.8 us -> 50.7 us (level)
  no operation moved by 1% of the time
where the time goes in v4:
time: 50.7 us; the launch traced here: 50.6 us
  Pallas kernels  49.9 us (98%)
  between operations  0.64 us (1%)
    pallas_call x1, Pallas kernels, body(): pl.pallas_call(functools.partial(mixer_kernel, (pieces, group_a, group_b,...  49 us

profile of v4, /device:TPU:1, one launch (start us, length us, event | category | flops | bytes accessed | tf_op | source)
XLA Modules:
  0.0 50.6 jit_solution(17384073033704830757)
XLA Ops:
  0.6 49.0 %mixer.1 = (bf16[128,512]{1,0:T(8,128)(2,1)S(1)}, bf16[128,512]{1,0:T(8,128)(2,1)S(1)}, bf16[128,512]{1,0:T(8,128)(2,1)S(1)}, bf16[128,512]{1,0:T(8,128)(2,1)S(1...) custom-call(f32[128,512]{1,0:T(8,128)} %refs_0_.1, bf16[128,512]{1,0:T(8,128)(2,1)} %refs_1_.1, ...), custom_call_target="tpu_custom_call" | custom-call | tf_op jit(solution)/shard_map/mixer/pallas_call | solution.py:472
  49.6 1.0 %store.1 = (bf16[128,512]{1,0:T(8,128)(2,1)}, bf16[128,512]{1,0:T(8,128)(2,1)}, bf16[128,512]{1,0:T(8,128)(2,1)}, bf16[128,512]{1,0:T(8,128)(2,1)}, f32[128,512]...) custom-call(bf16[128,512]{1,0:T(8,128)(2,1)S(1)} %get-tuple-element.21.refs_0_, ...), custom_call_target="tpu_custom_call" | custom-call | tf_op jit(solution)/shard_map/store/pallas_call | solution.py:507

commit v5 on v4

--- a/solution.py
+++ b/solution.py
@@ -169,7 +169,9 @@
 
     def to_pieces(slot, cb, block):
         per = LANES // OWN
-        src[slot, cb * per : (cb + 1) * per] = block.T.reshape(per, OWN, rows).astype(BF16)
+        src[slot, cb * per : (cb + 1) * per] = (
+            block.astype(BF16).T.astype(F32).reshape(per, OWN, rows).astype(BF16)
+        )
 
     def from_pieces(slot, cb):
         per = LANES // OWN
@@ -403,8 +405,9 @@
 
     sums = total_of(red2, group_b, SUM2)
     squares = sums[:, :channels] * sums[:, :channels]
-    square = jnp.sum(squares, keepdims=True) + jnp.sum(sums[:, channels:], keepdims=True)
-    nrm[...] = jnp.broadcast_to(square, nrm.shape)
+    square = sum(squares[:, b] for b in blocks) + sums[:, channels:]
+    square = jnp.sum(square, axis=0, keepdims=True)
+    nrm[...] = square
     exchange(nrm, nrmd, ch, chs, NORM, lambda peer: (me, peer))
     small_ref[...] = sums[:, :channels]
 
@@ -412,8 +415,9 @@
     for cb, cs in enumerate(blocks):
         lag_ref[:, cs] = from_pieces(5, cb)
 
-    norm_sq = total_of(nrmd, chs, NORM)
-    factor_ref[...] = limit / jnp.maximum(jnp.sqrt(norm_sq), limit)
+    norm_sq = jnp.sum(total_of(nrmd, chs, NORM), keepdims=True)
+    factor = limit / jnp.maximum(jnp.sqrt(norm_sq), limit)
+    factor_ref[...] = jnp.broadcast_to(factor, factor_ref.shape)
 
     wait_many(red1, group_a, ssem.at[SUM1])
     wait_many(red2, group_b, ssem.at[SUM2])
@@ -429,8 +433,6 @@
     near, far, (kern, short, skip, sem) = refs[:7], refs[7:14], refs[14:]
     lag_ref, small_ref, factor_ref = near[4:]
     copies = [pltpu.make_async_copy(a, b, sem.at[i]) for i, (a, b) in enumerate(zip(near[:4], far))]
-    for copy in copies:
-        copy.start()
     factor = factor_ref[0:1, 0:1]
     step = kern.shape[0] // 4
     for i in range(4):
@@ -438,6 +440,8 @@
         kern[here, :] = factor * lag_ref[here, :]
         copies.append(pltpu.make_async_copy(kern.at[here], far[4].at[here], sem.at[4 + i]))
         copies[-1].start()
+    for copy in copies[:4]:
+        copy.start()
     short[...] = factor * small_ref[0:3, :]
     skip[...] = (factor * small_ref[3:4, :]).reshape(skip.shape)
     for i, (a, b) in enumerate(((short, far[5]), (skip, far[6]))):

time: 50.7 us -> 50.8 us (level)
  no operation moved by 1% of the time
where the time goes in v5:
time: 50.8 us; the launch traced here: 50.7 us
  Pallas kernels  50 us (98%)
  between operations  0.64 us (1%)
    pallas_call x1, Pallas kernels, body(): pl.pallas_call(functools.partial(mixer_kernel, (pieces, group_a, group_b,...  49 us
    pallas_call x1, Pallas kernels, body(): pl.pallas_call(store_kernel, out_shape=[wide, wide, wide, wide, f32_wide,...  1.04 us

profile of v5, /device:TPU:1, one launch (start us, length us, event | category | flops | bytes accessed | tf_op | source)
XLA Modules:
  0.0 50.7 jit_solution(6498367986784265608)
XLA Ops:
  0.6 49.0 %mixer.1 = (bf16[128,512]{1,0:T(8,128)(2,1)S(1)}, bf16[128,512]{1,0:T(8,128)(2,1)S(1)}, bf16[128,512]{1,0:T(8,128)(2,1)S(1)}, bf16[128,512]{1,0:T(8,128)(2,1)S(1...) custom-call(f32[128,512]{1,0:T(8,128)} %refs_0_.1, bf16[128,512]{1,0:T(8,128)(2,1)} %refs_1_.1, ...), custom_call_target="tpu_custom_call" | custom-call | tf_op jit(solution)/shard_map/mixer/pallas_call | solution.py:476
  49.6 1.0 %store.1 = (bf16[128,512]{1,0:T(8,128)(2,1)}, bf16[128,512]{1,0:T(8,128)(2,1)}, bf16[128,512]{1,0:T(8,128)(2,1)}, bf16[128,512]{1,0:T(8,128)(2,1)}, f32[128,512]...) custom-call(bf16[128,512]{1,0:T(8,128)(2,1)S(1)} %get-tuple-element.21.refs_0_, ...), custom_call_target="tpu_custom_call" | custom-call | tf_op jit(solution)/shard_map/store/pallas_call | solution.py:511
